TPU v7x, 128 devices: a whole 4x4x4 slice. The times are simulated.
128 devices in a mesh: val: 4 (over z_lo, core), cond: 32 (over y, x, z_hi).
Axes of the slice: x: 4, y: 4, z: 4 (z_hi: 2, z_lo: 2; z = z_hi * 2 + z_lo), core: 2. Of those that a mesh axis runs over, the one named last changes fastest.
Arguments:
- valence_orbitals: bfloat16 [8, 96, 9216], P('val', 'cond'), may hold values from -6 to 6
- conduction_orbitals: bfloat16 [256, 96, 9216], P('cond'), may hold values from -6 to 6
- valence_energy: float32 [8], P('val'), may hold values from -14 to -5
- conduction_energy: float32 [256], P('cond'), may hold values from 0.5 to 40
- sphere_index: int32 [4096], replicated, may hold values from 0 to 884735, as said below
Outputs:
- polar_real: float32 [4096, 4096], P('cond', 'val')
- polar_imag: float32 [4096, 4096], P('cond', 'val')
Inputs may be any that keep to these rules, and one draw needn't show every extreme that they name: `sphere_index`: distinct flat indices (a * 96 + b) * 96 + e of the grid: the 4096 frequency vectors nearest the anchor, ties in length broken at random, listed in random order. Each component a, b, e, read as a frequency in -48 to 47, lies within -10 to 10.
All inputs are finite; a program needn't handle non-finite values.
Results may differ from a plain program's by a relative error of at most 0.0003.
Values may be sent and summed in bfloat16 or wider, within the bound.
No kernel may reach another device: no remote copies, remote signals or barrier semaphores. Data moves between devices by JAX's collectives and lax.ppermute only.
A program may use at most 320 MiB of HBM per device.

v0:
```python
import math

import jax
import jax.numpy as jnp
from jax import lax
from jax.sharding import PartitionSpec as P

NGRID = 96
KCUT = 10
NG = 4096


def twiddles(extent, cutoff):
    frequency = jnp.arange(2 * cutoff + 1, dtype=jnp.int32) - cutoff
    positions = jnp.arange(extent, dtype=jnp.int32)
    phases = positions[:, None] * (frequency[None, :] % extent) % extent
    angles = phases.astype(jnp.float32) * (2.0 * math.pi / extent)
    return (jnp.cos(angles), jnp.sin(angles))


def transform_yz(density, extent, cutoff):
    cosines, sine_part = twiddles(extent, cutoff)
    width = cosines.shape[1]
    table_zed = jnp.concatenate([cosines, -sine_part], axis=1)
    along_z = jnp.einsum("bxyz,zl->bxyl", density, table_zed, precision=lax.Precision.HIGHEST)
    table_yed = jnp.concatenate([cosines, sine_part], axis=1)
    products = jnp.einsum("bxyj,yl->bxlj", along_z, table_yed, precision=lax.Precision.HIGHEST)
    real_part = products[:, :, :width, :width] + products[:, :, width:, width:]
    imag_part = products[:, :, :width, width:] - products[:, :, width:, :width]
    return jnp.stack([real_part, imag_part], axis=1)


def finish_x(partial_value, extent, cutoff):
    cosines, sine_part = twiddles(extent, cutoff)
    width = cosines.shape[1]
    table_xed = jnp.concatenate([cosines, sine_part], axis=1)
    products = jnp.einsum(
        "bsxac,xl->bslac", partial_value, table_xed, precision=lax.Precision.HIGHEST
    )
    real_part = products[:, 0, :width] + products[:, 1, width:]
    imag_part = products[:, 1, :width] - products[:, 0, width:]
    factor = float(extent) ** (-1.5)
    count = partial_value.shape[0]
    return (real_part.reshape(count, -1) * factor, imag_part.reshape(count, -1) * factor)


def sphere_cells(sphere_index, extent, cutoff):
    side = 2 * cutoff + 1
    first = sphere_index // (extent * extent)
    second = sphere_index // extent % extent
    third = sphere_index % extent

    def folded(values):
        return jnp.where(values >= extent // 2, values - extent, values) + cutoff

    return (folded(first) * side + folded(second)) * side + folded(third)


def contract_pairs(row_side, col_side):
    return lax.dot_general(
        row_side, col_side, (((0,), (0,)), ((), ())), precision=lax.Precision.HIGHEST
    )


def per_device(
    valence_orbitals, conduction_orbitals, valence_energy, conduction_energy, sphere_index
):
    vcount = valence_orbitals.shape[0]
    ccount = conduction_orbitals.shape[0]
    block_rows = lax.all_gather(valence_orbitals, "cond", axis=1, tiled=True)
    planes = block_rows.shape[1]
    density = (
        block_rows.astype(jnp.float32)[:, None] * conduction_orbitals.astype(jnp.float32)[None]
    )
    density = density.reshape(vcount * ccount, planes, NGRID, NGRID)
    partial_value = transform_yz(density, NGRID, KCUT)
    real_part, imag_part = finish_x(partial_value, NGRID, KCUT)
    cells = sphere_cells(sphere_index, NGRID, KCUT)
    coefs = jnp.concatenate(
        [jnp.take(real_part, cells, axis=1), jnp.take(imag_part, cells, axis=1)], axis=1
    )
    weights = (2.0 / (valence_energy[:, None] - conduction_energy[None, :])).reshape(-1)
    cond_count = lax.axis_size("cond")
    val_count = lax.axis_size("val")
    rows = NG // cond_count
    cols = NG // val_count
    factor = float(vcount * val_count * ccount * cond_count) ** (-0.5)
    row_start = lax.axis_index("cond") * rows
    block_coef = lax.all_gather(coefs, "cond", axis=0, tiled=True)
    block_weight = lax.all_gather(weights, "cond", axis=0, tiled=True)
    row_real = lax.dynamic_slice_in_dim(block_coef, row_start, rows, 1)
    row_imag = lax.dynamic_slice_in_dim(block_coef, row_start + NG, rows, 1)
    row_side = jnp.concatenate([row_real, row_imag], axis=1) * block_weight[:, None]
    running = contract_pairs(row_side, block_coef)
    polar_real = running[:rows, :NG] + running[rows:, NG:]
    polar_imag = running[rows:, :NG] - running[:rows, NG:]
    polar_real, polar_imag = lax.psum((polar_real, polar_imag), "val")
    col_start = lax.axis_index("val") * cols
    polar_real = lax.dynamic_slice_in_dim(polar_real, col_start, cols, 1)
    polar_imag = lax.dynamic_slice_in_dim(polar_imag, col_start, cols, 1)
    return (polar_real * factor, polar_imag * factor)


def solution(mesh):
    placed = (P("val", "cond", None), P("cond", None, None), P("val"), P("cond"), P())
    return jax.shard_map(
        per_device,
        mesh=mesh,
        in_specs=placed,
        out_specs=(P("cond", "val"), P("cond", "val")),
        check_vma=False,
    )
```

profile of v0, /device:TPU:0, one launch (start us, length us, event | category | flops | bytes accessed | tf_op | source)
XLA Modules:
  0.0 822.1 jit_solution(12938597969930573149)
XLA Ops:
  8.0 15.7 %convert_element_type.18 = f32[8,96,9216]{2,1,0:T(8,128)} convert(bf16[8,96,9216]{2,1,0:T(8,128)(2,1)} %param.8) | non-fusion elementwise | flops 7077888 | bytes 42467328 | tf_op jit(solution)/shard_map/convert_element_type | solution.py:73
  23.8 69.1 %all-gather.3.cloned.1.call-done = bf16[2,96,9216]{2,0,1:T(2,128)(2,1)} async-done(((bf16[2,3,9216]{2,0,1:T(2,128)(2,1)}), bf16[2,96,9216]{2,0,1:T(2,128)(2,1)}) %all-gather.3.cloned.1.call-update) | async-done | bytes 3538960 | tf_op jit(solution)/shard_map/all_gather | solution.py:70
  92.9 5.7 copy_convert_fusion
  98.6 31.0 %broadcast_multiply_fusion = f32[2,8,96,9216]{3,2,1,0:T(8,128)} fusion(f32[8,96,9216]{2,1,0:T(8,128)} %convert_element_type.18, f32[2,96,9216]{2,1,0:T(8,128)} %copy_convert_fusion), kind=kLoop, calls=%fused_computation.4 | loop fusion | flops 14155776 | bytes 92012544 | tf_op jit(solution)/shard_map/mul | solution.py:73
  129.6 67.4 %mul.110 = f32[16,96,96,96]{3,2,1,0:T(8,128)} reshape(f32[2,8,96,9216]{3,2,1,0:T(8,128)} %broadcast_multiply_fusion) | data formatting | bytes 113246208 | tf_op jit(solution)/shard_map/mul | solution.py:73
  197.0 165.0 %fusion.19 = f32[16,96,96,42]{2,3,1,0:T(8,128)} fusion(f32[16,96,96,96]{3,2,1,0:T(8,128)} %mul.110, f32[96,21]{0,1:T(8,128)S(1)} %get-tuple-element.19, f32[96,21]{0,1:T(8,128)S(1)} %get-tuple-element.18), kind=kOutput, calls=%fused_computation.38 | convolution fusion | flops 7134515200 | bytes 81411840 | tf_op jit(solution)/shard_map/bxyz,zl->bxyl/dot_general | solution.py:25
  362.0 83.7 %fusion.2 = f32[16,96,42,42]{1,2,3,0:T(8,128)} fusion(f32[16,96,96,42]{2,3,1,0:T(8,128)} %fusion.19, f32[96,21]{0,1:T(8,128)S(1)} %get-tuple-element.19, f32[96,21]{0,1:T(8,128)S(1)} %get-tuple-element.17), kind=kOutput, calls=%fused_computation.5 | convolution fusion | flops 3121352704 | bytes 35626752 | tf_op jit(solution)/shard_map/bxyj,yl->bxlj/dot_general | solution.py:27
  445.7 11.2 %fusion.10 = (f32[16,1,96,21,21]{2,3,4,0,1:T(8,128)}, f32[16,1,96,21,21]{2,3,4,0,1:T(8,128)}) fusion(f32[16,96,42,42]{1,2,3,0:T(8,128)} %fusion.2), kind=kLoop, calls=%fused_computation.16 | loop fusion | flops 1354752 | bytes 16257024 | tf_op jit(solution)/shard_map/stack | solution.py:30
  456.9 4.0 pad_maximum_fusion
  460.9 8.7 %fusion.11 = f32[16,2,42,21,21]{2,4,3,1,0:T(8,128)} fusion(f32[16,2,96,21,21]{2,3,4,0,1:T(8,128)S(1)} %pad_maximum_fusion, f32[96,21]{0,1:T(8,128)S(1)} %get-tuple-element.19, f32[96,21]{0,1:T(8,128)S(1)} %get-tuple-element.17), kind=kOutput, calls=%fused_computation.18 | convolution fusion | flops 682799040 | bytes 7805952 | tf_op jit(solution)/shard_map/bsxac,xl->bslac/dot_general | solution.py:37
  469.6 11.3 %fusion.8 = (f32[16,1,21,21,21]{2,4,3,1,0:T(8,128)}, f32[16,1,21,21,21]{2,4,3,1,0:T(8,128)}) fusion(f32[16,2,42,21,21]{2,4,3,1,0:T(8,128)} %fusion.11), kind=kLoop, calls=%fused_computation.12 | loop fusion | flops 592704 | bytes 3556224 | tf_op jit(solution)/shard_map/mul | solution.py:44
  481.0 7.2 copy.36
  488.2 6.1 reshape.82
  494.3 7.2 copy.37
  501.5 6.1 reshape.83
  507.6 16.5 %gather_fusion = f32[4096,16]{1,0:T(8,128)} fusion(f32[16,9261]{0,1:T(8,128)} %reshape.82, s32[4096]{0:T(1024)S(1)} %broadcast_clamp_fusion), kind=kCustom, calls=%fused_computation.clone | custom fusion | bytes 540672 | tf_op jit(solution)/shard_map/jit(_take)/gather | solution.py:80
  524.1 16.4 %gather_fusion.1 = f32[4096,16]{1,0:T(8,128)} fusion(f32[16,9261]{0,1:T(8,128)} %reshape.83, s32[4096]{0:T(1024)S(1)} %broadcast_clamp_fusion), kind=kCustom, calls=%fused_computation.1.clone | custom fusion | bytes 540672 | tf_op jit(solution)/shard_map/jit(_take)/gather | solution.py:80
  540.5 3.5 select_bitcast_fusion.1
  549.4 92.6 %all-reduce = f32[512]{0:T(512)S(1)} all-reduce(f32[512]{0:T(512)S(1)} %dynamic-update-slice), channel_id=1, replica_groups=mesh['val'=4,'cond'=32] {'cond'}, use_global_device_ids=true, to_apply=%add | all-reduce | flops 512 | bytes 4096
  642.0 60.0 %all-gather.5.cloned.1.call-done = f32[512,8192]{1,0:T(8,128)} async-done(((f32[16,8192]{1,0:T(8,128)}), f32[512,8192]{1,0:T(8,128)}) %all-gather.5.cloned.1.call-update) | async-done | bytes 16777232 | tf_op jit(solution)/shard_map/all_gather | solution.py:89
  703.1 17.7 %fusion.14 = f32[256,8192]{1,0:T(8,128)S(1)} fusion(f32[512,8192]{1,0:T(8,128)} %all-gather.5.cloned.1.call-done, f32[512,128]{1,0:T(8,128)S(1)} %get-tuple-element.8, f32[512,128]{1,0:T(8,128)S(1)} %get-tuple-element.7, f32[512]{0:T(512)S(1)} %all-reduce), kind=kOutput, calls=%fused_computation.25 | convolution fusion | flops 12885164032 | bytes 25692160 | tf_op jit(solution)/shard_map/dot_general | solution.py:60
  720.8 2.5 slice_subtract_fusion.2
  723.3 89.7 %all-reduce.4.cloned.1.call-done = (f32[128,4096]{1,0:T(8,128)}, f32[128,4096]{1,0:T(8,128)}) async-done(((f32[128,4096]{1,0:T(8,128)}, f32[128,4096]{1,0:T(8,128)}), (f32[128,4096]{1,0:T(8,128)}, f32[128,4096]{1,0:T(8,128)})) %all-reduce.4.cloned.1.call-update) | async-done | bytes 4194320 | tf_op jit(solution)/shard_map/psum | solution.py:97
  813.0 2.3 dynamic-slice_multiply_fusion
  (27 shorter events, 6.7 us)
Async XLA Ops:
  7.2 85.7 %all-gather.3.cloned.1.call-start = ((), (), s32[]{:S(2)}) async-start(), calls=%async_computation | async-start | bytes 3649536 | tf_op jit(solution)/shard_map/all_gather | solution.py:70
  7.9 15.7 %copy-start = (s32[4096]{0:T(1024)S(1)}, s32[4096]{0:T(1024)}, u32[]{:S(2)}) copy-start(s32[4096]{0:T(1024)} %param.11) | copy-start | bytes 49156
  7.9 694.1 %all-gather.5.cloned.1.call-start = ((), (), s32[]{:S(2)}) async-start(), calls=%async_computation.1 | async-start | bytes 17301504 | tf_op jit(solution)/shard_map/all_gather | solution.py:89
  544.0 3.7 copy-start.1
  544.0 3.7 copy-start.2
  544.0 3.9 copy-start.3
  547.7 265.3 %all-reduce.4.cloned.1.call-start = ((), (), s32[]{:S(2)}) async-start(), calls=%async_computation.2 | async-start | bytes 8388608 | tf_op jit(solution)/shard_map/psum | solution.py:97
Sparse Core Ops, SparseCore 0:
  11.0 81.8 all-gather.2
  547.8 154.1 all-gather.4
  723.5 89.5 all-reduce.3
where the time goes:
time: 828 us; the launch traced here: 822 us
  matrix products  275 us (33%)
  waiting for transfers between devices  219 us (26%)
  local copies, waits for them, and re-layouts  132 us (16%)
  blocking collectives  92.6 us (11%)
  other arithmetic  88.3 us (11%)
  between operations  14.8 us (2%)
    dot_general x1, matrix products, transform_yz(): jnp.einsum('bxyz,zl->bxyl', density, table_zed, precision=lax.Precision.H...  165 us
    unnamed x1, blocking collectives  92.6 us
    psum x1, waiting for transfers between devices, per_device(): polar_real, polar_imag = lax.psum((polar_real, polar_imag), 'val')  89.7 us
    dot_general x1, matrix products, transform_yz(): jnp.einsum('bxyj,yl->bxlj', along_z, table_yed, precision=lax.Precision.H...  83.7 us
    all_gather x1, waiting for transfers between devices, per_device(): block_rows = lax.all_gather(valence_orbitals, 'cond', axis=1, tiled=True)  69.1 us
    mul x1, local copies, waits for them, and re-layouts, per_device(): block_rows.astype(jnp.float32)[:, None]  67.4 us
    all_gather x1, waiting for transfers between devices, per_device(): block_coef = lax.all_gather(coefs, 'cond', axis=0, tiled=True)  60 us
    mul x1, other arithmetic, per_device(): block_rows.astype(jnp.float32)[:, None]  31 us
  transfers between devices with their start and end apart: 3, of which 3 were waited for; matrix products, arithmetic and copies ran while one was open for 2% of the time, Pallas kernels for 0%

commit v1 on v0

v1 whole, which is shorter than its diff:
```python
import math

import jax
import jax.numpy as jnp
import numpy as np
from jax import lax
from jax.experimental import pallas as pl
from jax.experimental.pallas import tpu as pltpu
from jax.sharding import Mesh, PartitionSpec as P

NGRID = 96
KCUT = 10
NG = 4096
SIDE = 2 * KCUT + 1
HALF = NGRID // 2
PLANE = NGRID * NGRID
FOLD = PLANE // 2
ELEN = KCUT + 1
CHUNK = 512
PAIRS = 16
CODES = 32767.0
LOG2 = math.log(2.0)
VAL = ("zl", "core")
COND = ("y", "x", "zh")


def split_np(table):
    high = table.astype(jnp.bfloat16)
    low = (table - high.astype(np.float64)).astype(jnp.bfloat16)
    return high, low


def plane_tables():
    phase_y = np.arange(HALF)[:, None, None, None]
    phase_z = np.arange(NGRID)[None, :, None, None]
    zed = np.arange(ELEN)[None, None, None, :]
    blocks = []
    for first in (-KCUT, -KCUT + 1):
        yed = np.arange(first, KCUT + 1, 2)[None, None, :, None]
        angle = (yed * phase_y + zed * phase_z) % NGRID * (2.0 * math.pi / NGRID)
        angle = angle.reshape(FOLD, -1)
        table = np.zeros((FOLD, 256))
        table[:, : angle.shape[1]] = np.cos(angle)
        table[:, 128 : 128 + angle.shape[1]] = -np.sin(angle)
        blocks.append(table)
    even_high, even_low = split_np(blocks[0])
    odd_high, odd_low = split_np(blocks[1])
    return even_high, even_low, odd_high, odd_low


def line_tables():
    freq = np.arange(-KCUT, KCUT + 1)[:, None]
    angle = freq * np.arange(NGRID)[None, :] % NGRID * (2.0 * math.pi / NGRID)
    parts = np.stack([np.cos(angle), np.sin(angle)])
    eye = np.eye(PAIRS)
    table = np.einsum("sax,pq->sapqx", parts, eye)
    return split_np(table.reshape(2 * SIDE * PAIRS, PAIRS * NGRID))


def dot32(left, right):
    return lax.dot_general(
        left, right, (((1,), (0,)), ((), ())), preferred_element_type=jnp.float32
    )


def split(value):
    high = value.astype(jnp.bfloat16)
    low = (value - high.astype(jnp.float32)).astype(jnp.bfloat16)
    return high, low


def plane_kernel(v0_ref, v1_ref, c0_ref, c1_ref, eh_ref, el_ref, oh_ref, ol_ref, out_ref):
    first = pl.program_id(0) == 0

    @pl.when(first)
    def _():
        out_ref[...] = jnp.zeros_like(out_ref)

    vcount = v0_ref.shape[0]
    ccount = c0_ref.shape[0]
    group = 4
    for v in range(vcount):
        v0 = v0_ref[v].astype(jnp.float32)[None]
        v1 = v1_ref[v].astype(jnp.float32)[None]
        for c in range(0, ccount, group):
            d0 = v0 * c0_ref[c : c + group].astype(jnp.float32)
            d1 = v1 * c1_ref[c : c + group].astype(jnp.float32)
            rows = group * d0.shape[1]
            at = (v * ccount + c) * d0.shape[1]
            for which, value in enumerate((d0 + d1, d0 - d1)):
                high, low = split(value.reshape(rows, CHUNK))
                th = (eh_ref, oh_ref)[which][...]
                tl = (el_ref, ol_ref)[which][...]
                part = dot32(high, th) + dot32(low, th) + dot32(high, tl)
                out_ref[at : at + rows, which * 256 : which * 256 + 256] += part


def plane_transform(valence, conduction, tables):
    vcount, planes, _ = valence.shape
    ccount = conduction.shape[0]
    steps = FOLD // CHUNK
    rows = vcount * ccount * planes
    vspec = lambda off: pl.BlockSpec((vcount, planes, CHUNK), lambda k: (0, 0, k + off))
    cspec = lambda off: pl.BlockSpec((ccount, planes, CHUNK), lambda k: (0, 0, k + off))
    tspec = pl.BlockSpec((CHUNK, 256), lambda k: (k, 0))
    return pl.pallas_call(
        plane_kernel,
        grid=(steps,),
        in_specs=[vspec(0), vspec(steps), cspec(0), cspec(steps)] + [tspec] * 4,
        out_specs=pl.BlockSpec((rows, 512), lambda k: (0, 0)),
        out_shape=jax.ShapeDtypeStruct((rows, 512), jnp.float32),
        compiler_params=pltpu.CompilerParams(vmem_limit_bytes=56 * 2**20),
        cost_estimate=pl.CostEstimate(
            flops=rows * FOLD * 512 * 6, bytes_accessed=40 * 2**20, transcendentals=0
        ),
        name="plane_transform",
    )(valence, valence, conduction, conduction, *tables)


def line_kernel(
    y_ref, th_ref, tl_ref, lane_ref, freq_ref, sign_ref, gain_ref, cols_ref, rows_ref, step_ref,
    fh_ref, fl_ref, coef_ref,
):
    high, low = split(y_ref[...])
    th = th_ref[...]
    both = dot32(th, high) + dot32(th, low) + dot32(tl_ref[...], high)
    rows = SIDE * PAIRS
    cosine, sine = both[:rows], both[rows:]
    for par in range(2):
        at = par * 256
        real = cosine[:, at : at + 128] + sine[:, at + 128 : at + 256]
        imag = cosine[:, at + 128 : at + 256] - sine[:, at : at + 128]
        lanes = slice(par * 128, par * 128 + 128)
        fh_ref[:rows, lanes], fl_ref[:rows, lanes] = split(real)
        fh_ref[rows:, lanes], fl_ref[rows:, lanes] = split(imag)
    width = 512
    gain = gain_ref[...]

    def pick(tile, largest):
        cols = pl.ds(pl.multiple_of(tile * width, width), width)
        lane = lane_ref[:, cols]
        onehot = lax.broadcasted_iota(jnp.int32, (256, width), 0) == lane
        onehot = onehot.astype(jnp.float32).astype(jnp.bfloat16)
        freq = freq_ref[:, cols]
        picked = dot32(fh_ref[...], onehot) + dot32(fl_ref[...], onehot)
        for part in range(2):
            total = jnp.zeros((PAIRS, width), jnp.float32)
            for a in range(SIDE):
                at = part * rows + a * PAIRS
                total = jnp.where(freq == a, picked[at : at + PAIRS], total)
            total = total * gain
            if part == 1:
                total = total * sign_ref[:, cols]
            coef_ref[part * PAIRS : (part + 1) * PAIRS, cols] = total
            largest = jnp.maximum(largest, jnp.max(jnp.abs(total), axis=1, keepdims=True))
        return largest

    largest = lax.fori_loop(0, NG // width, pick, jnp.zeros((PAIRS, 1), jnp.float32))
    usable = largest > 1e-30
    step = jnp.ceil(jnp.log(jnp.where(usable, largest, 1.0) * (1.0 / CODES)) * (1.0 / LOG2))
    step_ref[...] = jnp.broadcast_to(step, step_ref.shape)
    inverse = jnp.where(usable, jnp.exp(step * -LOG2), 0.0)
    inverse = jnp.concatenate([inverse, inverse])
    for block in range(32):
        codes = jnp.round(coef_ref[:, block * 128 : (block + 1) * 128] * inverse)
        codes = jnp.clip(codes, -CODES, CODES).astype(jnp.int32).astype(jnp.int16)
        rows_ref[block] = codes
        cols_ref[block // 8, :, block % 8 * 128 : block % 8 * 128 + 128] = codes


def line_transform(planes, tables, slots, gain):
    rows = 2 * SIDE * PAIRS
    return pl.pallas_call(
        line_kernel,
        out_shape=(
            jax.ShapeDtypeStruct((4, 2 * PAIRS, NG // 4), jnp.int16),
            jax.ShapeDtypeStruct((32, 2 * PAIRS, NG // 32), jnp.int16),
            jax.ShapeDtypeStruct((PAIRS, 128), jnp.float32),
        ),
        scratch_shapes=[pltpu.VMEM((rows, 256), jnp.bfloat16)] * 2
        + [pltpu.VMEM((2 * PAIRS, NG), jnp.float32)],
        compiler_params=pltpu.CompilerParams(vmem_limit_bytes=48 * 2**20),
        cost_estimate=pl.CostEstimate(
            flops=rows * (PAIRS * NGRID * 512 * 6 + 256 * NG * 4),
            bytes_accessed=8 * 2**20,
            transcendentals=0,
        ),
        name="line_transform",
    )(planes, *tables, *slots, gain)


def pair_kernel(cols_ref, rows_ref, scale_ref, real_ref, imag_ref, total_ref):
    step = pl.program_id(0)
    depth = cols_ref.shape[0]
    rows = rows_ref.shape[1]
    row = rows_ref[...].astype(jnp.float32) * scale_ref[...]
    block = row.reshape(depth // (2 * PAIRS), 2, PAIRS, rows)
    turned = jnp.concatenate([block[:, 1:], -block[:, :1]], axis=1).reshape(depth, rows)
    rh, rl = split(jnp.concatenate([row, turned], axis=1))
    code = cols_ref[...].astype(jnp.int32)
    top = jnp.right_shift(code + 128, 8) * 256
    high = top.astype(jnp.float32).astype(jnp.bfloat16)
    low = (code - top).astype(jnp.float32).astype(jnp.bfloat16)

    def contract(left, right):
        return lax.dot_general(
            left, right, (((0,), (0,)), ((), ())), preferred_element_type=jnp.float32
        )

    part = contract(rh, high) + contract(rl, high) + contract(rh, low)

    @pl.when(step == 0)
    def _():
        total_ref[...] = part

    @pl.when(step > 0)
    def _():
        total_ref[...] += part

    @pl.when(step == pl.num_programs(0) - 1)
    def _():
        real_ref[...] = total_ref[:rows]
        imag_ref[...] = total_ref[rows:]


def pair_product(cols, rows, scale):
    depth = 512
    count, width = cols.shape
    height = rows.shape[1]
    shape = jax.ShapeDtypeStruct((height, width), jnp.float32)
    spec = lambda size: pl.BlockSpec((depth, size), lambda k: (k, 0))
    out = pl.BlockSpec((height, width), lambda k: (0, 0))
    return pl.pallas_call(
        pair_kernel,
        grid=(count // depth,),
        in_specs=[spec(width), spec(height), spec(1)],
        out_specs=(out, out),
        out_shape=(shape, shape),
        scratch_shapes=[pltpu.VMEM((2 * height, width), jnp.float32)],
        compiler_params=pltpu.CompilerParams(vmem_limit_bytes=48 * 2**20),
        cost_estimate=pl.CostEstimate(
            flops=6 * 2 * height * width * count, bytes_accessed=12 * 2**20, transcendentals=0
        ),
        name="pair_product",
    )(cols, rows, scale)


def sphere_slots(sphere_index):
    def folded(values):
        return jnp.where(values >= HALF, values - NGRID, values)

    first = folded(sphere_index // PLANE)
    second = folded(sphere_index // NGRID % NGRID)
    third = folded(sphere_index % NGRID)
    flip = third < 0
    sign = jnp.where(flip, -1, 1)
    first, second, third = first * sign, second * sign, third * sign
    even = second % 2 == 0
    lane = jnp.where(
        even, (second + KCUT) // 2 * ELEN + third, 128 + (second + KCUT - 1) // 2 * ELEN + third
    )
    row = lambda value: value.reshape(1, NG)
    return row(lane), row(first + KCUT), row(sign.astype(jnp.float32))


def gather_planes(orbitals):
    count = orbitals.shape[0]
    mine = orbitals.reshape(-1, 128).astype(jnp.float32)
    rows = mine.shape[0]
    largest = jnp.max(jnp.abs(mine))
    power = jnp.where(largest > 0.0, jnp.ceil(jnp.log2(jnp.where(largest > 0.0, largest, 1.0))), 0.0)
    power = jnp.maximum(power, -100.0)
    packed = jnp.concatenate(
        [mine * jnp.exp2(-power), jnp.broadcast_to(power, (8, 128))]
    ).astype(jnp.float16)
    packed = lax.all_gather(packed, "zh", axis=0)
    packed = lax.all_gather(packed, ("y", "x"), axis=0)
    values = packed[:, :, :rows].astype(jnp.float32)
    values = values * jnp.exp2(packed[:, :, rows:rows + 1, :1].astype(jnp.float32))
    values = values.astype(jnp.bfloat16).reshape(32, count, -1, 72, 128)
    return jnp.swapaxes(values, 0, 1).reshape(count, NGRID, PLANE)


def columns_of_all(coded):
    twice = jnp.broadcast_to(coded, (2,) + coded.shape).reshape((8,) + coded.shape[1:])
    line = lax.all_to_all(twice, ("zh",) + VAL, 0, 0, tiled=True)
    return lax.all_gather(line, ("y", "x"), axis=0).reshape(-1, coded.shape[-1])


def rows_of_all(coded, steps):
    height, rows = coded.shape[1:]
    steps = jnp.pad(steps[:, 0].astype(jnp.int16)[None], ((0, 7), (0, rows - PAIRS)))
    sent = jnp.concatenate([coded, jnp.broadcast_to(steps, (32, 8, rows))], axis=1)
    sent = jnp.broadcast_to(sent, (4,) + sent.shape).reshape((128,) + sent.shape[1:])
    got = lax.all_to_all(sent, VAL + COND, 0, 0, tiled=True)
    got = got.reshape(4, 16, 2, height + 8, rows).transpose(1, 2, 0, 3, 4)
    scale = jnp.exp2(2.0 * got[..., height, :PAIRS].astype(jnp.float32))
    scale = jnp.concatenate([scale, scale], axis=-1).reshape(-1, 1)
    return got[..., :height, :].reshape(-1, rows), -scale


def per_device(
    valence_orbitals, conduction_orbitals, valence_energy, conduction_energy, sphere_index
):
    slots = sphere_slots(sphere_index)
    weights = 2.0 / (conduction_energy[None, :] - valence_energy[:, None])
    gain = jnp.sqrt(weights * 2048.0**-0.5) * float(NGRID) ** -1.5
    valence = gather_planes(valence_orbitals)
    planes = plane_transform(valence, conduction_orbitals, plane_tables())
    cols, rows, steps = line_transform(planes, line_tables(), slots, gain.reshape(-1, 1))
    rows, scale = rows_of_all(rows, steps)
    return pair_product(columns_of_all(cols), rows, scale)


def solution(mesh):
    names = ("zl", "core", "y", "x", "zh")
    fine = Mesh(mesh.devices.reshape(2, 2, 4, 4, 2), names)
    placed = (P(VAL, COND, None), P(COND, None, None), P(VAL), P(COND), P())
    return jax.shard_map(
        per_device,
        mesh=fine,
        in_specs=placed,
        out_specs=(P(COND, VAL), P(COND, VAL)),
        check_vma=False,
    )
```

time: 828 us -> 207 us (0.25)
  matrix products: 275 us -> 0 us
  waiting for transfers between devices: 219 us -> 10.2 us
  local copies, waits for them, and re-layouts: 132 us -> 16.5 us
  other arithmetic: 88.3 us -> 7.34 us
  Pallas kernels: 0 us -> 55.1 us
  between operations: 14.8 us -> 2.15 us
  blocking collectives: 92.6 us -> 104 us
  starting transfers between devices: 0.12 us -> 10.3 us
    dot_general x4 -> x0, matrix products: 275 us -> none  [the longest x1 165 us: transform_yz(): jnp.einsum('bxyz,zl->bxyl', density, table_zed, precision=lax.Precision.H...]
    all_gather x2 -> x0, waiting for transfers between devices: 129 us -> none  [the longest x1 69.1 us: per_device(): block_rows = lax.all_gather(valence_orbitals, 'cond', axis=1, tiled=True)]
    all_gather x0 -> x3, blocking collectives: none -> 104 us  [the longest x1 64.3 us: columns_of_all(): return lax.all_gather(line, ('y', 'x'), axis=0).reshape(-1, coded.shape[-1])]
    mul x5 -> x3, local copies, waits for them, and re-layouts: 94.1 us -> 0.27 us  [the longest x1 0.1 us: gather_planes(): mine * jnp.exp2(-power)]
    unnamed x1 -> x0, blocking collectives: 92.6 us -> none
    psum x1 -> x0, waiting for transfers between devices: 89.7 us -> none  [per_device(): polar_real, polar_imag = lax.psum((polar_real, polar_imag), 'val')]
    pallas_call x0 -> x3, Pallas kernels: none -> 55.1 us  [the longest x1 30.9 us: plane_transform(): pl.pallas_call(plane_kernel, grid=(steps,), in_specs=[vspec(0), vspec(ste...]
    mul x3 -> x2, other arithmetic: 44.6 us -> 0.76 us  [the longest x1 0.75 us: per_device(): gain = jnp.sqrt(weights * 2048.0 ** (-0.5)) * float(NGRID) ** (-1.5)]
  transfers between devices with their start and end apart: 3 -> 2, of which waited for: 3 -> 1; matrix products, arithmetic and copies ran while one was open for 2% -> 0% of each run, Pallas kernels for 0% -> 0%
where the time goes in v1:
time: 207 us; the launch traced here: 206 us
  blocking collectives  104 us (50%)
  Pallas kernels  55.1 us (27%)
  local copies, waits for them, and re-layouts  16.5 us (8%)
  starting transfers between devices  10.3 us (5%)
  waiting for transfers between devices  10.2 us (5%)
  other arithmetic  7.34 us (4%)
  between operations  2.15 us (1%)
    all_gather x1, blocking collectives, columns_of_all(): return lax.all_gather(line, ('y', 'x'), axis=0).reshape(-1, coded.shape[-1])  64.3 us
    all_gather x1, blocking collectives, gather_planes(): packed = lax.all_gather(packed, ('y', 'x'), axis=0)  32.4 us
    pallas_call x1, Pallas kernels, plane_transform(): pl.pallas_call(plane_kernel, grid=(steps,), in_specs=[vspec(0), vspec(ste...  30.9 us
    pallas_call x1, Pallas kernels, pair_product(): pl.pallas_call(pair_kernel, grid=(count // depth,), in_specs=[spec(width)...  13.7 us
    pallas_call x1, Pallas kernels, line_transform(): pl.pallas_call(line_kernel, out_shape=(jax.ShapeDtypeStruct((4, 2 * PAIRS...  10.5 us
    all_to_all x1, waiting for transfers between devices, columns_of_all(): line = lax.all_to_all(twice, ('zh',) + VAL, 0, 0, tiled=True)  10.2 us
    all_gather x1, blocking collectives, gather_planes(): packed = lax.all_gather(packed, 'zh', axis=0)  7.72 us
    all_to_all x1, starting transfers between devices, rows_of_all(): got = lax.all_to_all(sent, VAL + COND, 0, 0, tiled=True)  6.24 us
  transfers between devices with their start and end apart: 2, of which 1 were waited for; matrix products, arithmetic and copies ran while one was open for 0% of the time, Pallas kernels for 0%

profile of v1, /device:TPU:0, one launch (start us, length us, event | category | flops | bytes accessed | tf_op | source)
XLA Modules:
  0.0 205.9 jit_solution(11486998064125723944)
XLA Ops:
  0.6 1.7 fusion
  3.8 0.8 sqrt_multiply_fusion
  4.6 0.8 select_convert_fusion
  5.4 1.0 fusion.1
  6.7 7.7 %all-gather = f16[880,128]{1,0:T(8,128)(2,1)S(1)} all-gather(f16[440,128]{1,0:T(8,128)(2,1)S(1)} %concatenate.9), channel_id=2, replica_groups=mesh['zl'=2,'core'=2,'y'=4,'x'=4,'zh'=2] {'zh'}, dimensions={0}, use_global_device_ids=true | all-gather | bytes 337920 | tf_op jit(solution)/shard_map/all_gather | solution.py:276
  14.4 32.4 %all-gather.5 = f16[32,440,128]{2,1,0:T(8,128)(2,1)S(1)} all-gather(f16[2,440,128]{2,1,0:T(8,128)(2,1)S(1)} %bitcast.34), channel_id=3, replica_groups=mesh['zl'=2,'core'=2,'y'=4,'x'=4,'zh'=2] {'y','x'}, dimensions={0}, use_global_device_ids=true | all-gather | bytes 3829760 | tf_op jit(solution)/shard_map/all_gather | solution.py:277
  46.8 1.8 copy-done.2
  48.8 2.8 %multiply_convert_fusion = bf16[16,2,432,128]{3,2,1,0:T(8,128)(2,1)S(1)} fusion(f16[16,2,440,128]{3,2,1,0:T(8,128)(2,1)} %bitcast.28, f32[16,2]{1,0:T(8,128)S(1)} %copy.33), kind=kLoop, calls=%fused_computation | loop fusion | flops 5308416 | bytes 7078016 | tf_op jit(solution)/shard_map/convert_element_type | solution.py:280
  51.5 2.4 %copy.34 = bf16[2,32,3,72,128]{4,3,2,1,0:T(8,128)(2,1)} copy(bf16[2,32,3,72,128]{4,3,2,0,1:T(8,128)(2,1)S(1)} %bitcast.29) | data formatting | bytes 7077888 | tf_op jit(solution)/shard_map/transpose | solution.py:281
  53.9 6.1 %reshape.111.v0_ref.v1_ref = bf16[2,96,9216]{2,1,0:T(8,128)(2,1)} reshape(bf16[2,32,3,72,128]{4,3,2,1,0:T(8,128)(2,1)} %copy.34) | data formatting | bytes 7077888 | tf_op jit(solution)/shard_map/reshape | solution.py:281
  60.0 30.9 %plane_transform.1.y_ref = f32[1536,512]{1,0:T(8,128)} custom-call(bf16[2,96,9216]{2,1,0:T(8,128)(2,1)} %reshape.111.v0_ref.v1_ref, bf16[2,96,9216]{2,1,0:T(8,128)(2,1)} %reshape.111.v0_ref.v1_ref, bf16[8,96,9216]{2,1,0:T(8,128)(2,1)} %c1_ref.1, bf16[8,96,9216]{2,1,0:T(8,128)(2,1)} %c1_ref.1, bf16[4608,256]{1,0:T(8,128)(2,1)} %constant.112.clone.eh_ref, ...), custom_call_target="tpu_custom_call" | custom-call | flops 21743271936 | bytes 41943040 | tf_op jit(solution)/shard_map/plane_transform/pallas_call | solution.py:106
  90.9 10.5 %line_transform.1 = (s16[4,32,1024]{2,1,0:T(8,128)(2,1)S(1)}, s16[32,32,128]{2,1,0:T(8,128)(2,1)S(1)}, f32[16,128]{1,0:T(8,128)S(1)}) custom-call(f32[1536,512]{1,0:T(8,128)} %plane_transform.1.y_ref, bf16[672,1536]{1,0:T(8,128)(2,1)S(1)} %copy-done.1, bf16[672,1536]{1,0:T(8,128)(2,1)S(1)} %copy-done, s32[1,4096]{1,0:T(1,128)S(1)} %bitcast.26, ...), custom_call_target="tpu_custom_call" | custom-call | flops 5989466112 | bytes 8388608 | tf_op jit(solution)/shard_map/line_transform/pallas_call | solution.py:173
  101.4 0.9 broadcast_in_dim.10
  102.3 4.0 %all-to-all-start = ((s16[8,32,1024]{2,1,0:T(8,128)(2,1)}), s16[8,32,1024]{2,1,0:T(8,128)(2,1)S(1)}, u32[]{:S(2)}, u32[]{:S(2)}) async-start(s16[8,32,1024]{2,1,0:T(8,128)(2,1)} %bitcast.8), calls=%async_computation | async-start | bytes 1048576 | tf_op jit(solution)/shard_map/all_to_all | solution.py:286
  106.3 0.1 fusion.19
  106.5 10.2 %all-to-all-done = s16[8,32,1024]{2,1,0:T(8,128)(2,1)S(1)} async-done(((s16[8,32,1024]{2,1,0:T(8,128)(2,1)}), s16[8,32,1024]{2,1,0:T(8,128)(2,1)S(1)}, u32[]{:S(2)}, u32[]{:S(2)}) %all-to-all-start) | async-done | bytes 524320 | tf_op jit(solution)/shard_map/all_to_all | solution.py:286
  116.6 1.3 broadcast_in_dim.19
  118.0 6.2 %all-to-all-start.1 = ((s16[128,40,128]{2,1,0:T(8,128)(2,1)}), s16[128,40,128]{2,1,0:T(8,128)(2,1)S(1)}, u32[]{:S(2)}, u32[]{:S(2)}) async-start(s16[128,40,128]{2,1,0:T(8,128)(2,1)} %bitcast.10), calls=%async_computation.1 | async-start | bytes 2621440 | tf_op jit(solution)/shard_map/all_to_all | solution.py:295
  124.2 64.3 %all-gather.6 = s16[128,32,1024]{2,1,0:T(8,128)(2,1)} all-gather(s16[8,32,1024]{2,1,0:T(8,128)(2,1)S(1)} %all-to-all-done), channel_id=4, replica_groups=mesh['zl'=2,'core'=2,'y'=4,'x'=4,'zh'=2] {'y','x'}, dimensions={0}, use_global_device_ids=true | all-gather | bytes 8912896 | tf_op jit(solution)/shard_map/all_gather | solution.py:287
  188.6 0.3 copy.42
  188.9 0.2 slice.24
  189.2 0.7 copy.37
  190.0 2.2 %neg.11.scale_ref = f32[4096,1]{1,0:T(8,128)S(1)} reshape(f32[16,2,4,32]{3,2,1,0:T(4,128)S(1)} %copy.38) | data formatting | bytes 32768 | tf_op jit(solution)/shard_map/neg | solution.py:299
  192.2 13.7 %pair_product.1 = (f32[128,1024]{1,0:T(8,128)}, f32[128,1024]{1,0:T(8,128)}) custom-call(s16[4096,1024]{1,0:T(8,128)(2,1)} %bitcast.30, s16[4096,128]{1,0:T(8,128)(2,1)S(1)} %bitcast.23, f32[4096,1]{1,0:T(8,128)S(1)} %neg.11.scale_ref), custom_call_target="tpu_custom_call" | custom-call | flops 6442450944 | bytes 12582912 | tf_op jit(solution)/shard_map/pair_product/pallas_call | solution.py:233
  (20 shorter events, 0.7 us)
Async XLA Ops:
  46.8 1.8 copy-start.2
  60.0 30.9 %copy-start = (bf16[672,1536]{1,0:T(8,128)(2,1)S(1)}, bf16[672,1536]{1,0:T(8,128)(2,1)}, u32[]{:S(2)}) copy-start(bf16[672,1536]{1,0:T(8,128)(2,1)} %constant.117.clone.tl_ref) | copy-start | bytes 6193156
  60.0 30.9 %copy-start.1 = (bf16[672,1536]{1,0:T(8,128)(2,1)S(1)}, bf16[672,1536]{1,0:T(8,128)(2,1)}, u32[]{:S(2)}) copy-start(bf16[672,1536]{1,0:T(8,128)(2,1)} %constant.116.clone.th_ref) | copy-start | bytes 6193156
  102.3 14.4 %all-to-all-start = ((s16[8,32,1024]{2,1,0:T(8,128)(2,1)}), s16[8,32,1024]{2,1,0:T(8,128)(2,1)S(1)}, u32[]{:S(2)}, u32[]{:S(2)}) async-start(s16[8,32,1024]{2,1,0:T(8,128)(2,1)} %bitcast.8), calls=%async_computation | async-start | bytes 1048576 | tf_op jit(solution)/shard_map/all_to_all | solution.py:286
  118.0 70.6 %all-to-all-start.1 = ((s16[128,40,128]{2,1,0:T(8,128)(2,1)}), s16[128,40,128]{2,1,0:T(8,128)(2,1)S(1)}, u32[]{:S(2)}, u32[]{:S(2)}) async-start(s16[128,40,128]{2,1,0:T(8,128)(2,1)} %bitcast.10), calls=%async_computation.1 | async-start | bytes 2621440 | tf_op jit(solution)/shard_map/all_to_all | solution.py:295

commit v2 on v1

v2 whole, which is shorter than its diff:
```python
import math

import jax
import jax.numpy as jnp
import numpy as np
from jax import lax
from jax.experimental import pallas as pl
from jax.experimental.pallas import tpu as pltpu
from jax.sharding import Mesh, PartitionSpec as P

NGRID = 96
KCUT = 10
NG = 4096
SIDE = 2 * KCUT + 1
HALF = NGRID // 2
PLANE = NGRID * NGRID
FOLD = PLANE // 2
ELEN = KCUT + 1
CHUNK = 512
PAIRS = 16
GROUP = 8
ROWS = 176
CODES = 32767.0
LOG2 = math.log(2.0)
VAL = ("zl", "core")
COND = ("y", "x", "zh")


def split_np(table):
    high = table.astype(jnp.bfloat16)
    low = (table - high.astype(np.float64)).astype(jnp.bfloat16)
    return high, low


def plane_tables():
    phase_y = np.arange(HALF)[:, None, None, None]
    phase_z = np.arange(NGRID)[None, :, None, None]
    zed = np.arange(ELEN)[None, None, None, :]
    blocks = []
    for first in (-KCUT, -KCUT + 1):
        yed = np.arange(first, KCUT + 1, 2)[None, None, :, None]
        angle = (yed * phase_y + zed * phase_z) % NGRID * (2.0 * math.pi / NGRID)
        angle = angle.reshape(FOLD, -1)
        table = np.zeros((FOLD, 256))
        table[:, : angle.shape[1]] = np.cos(angle)
        table[:, 128 : 128 + angle.shape[1]] = -np.sin(angle)
        blocks.append(table)
    even_high, even_low = split_np(blocks[0])
    odd_high, odd_low = split_np(blocks[1])
    return even_high, even_low, odd_high, odd_low


def line_tables():
    freq = np.arange(-KCUT, KCUT + 1)[:, None]
    angle = freq * np.arange(NGRID)[None, :] % NGRID * (2.0 * math.pi / NGRID)
    parts = np.stack([np.cos(angle), np.sin(angle)])
    eye = np.eye(GROUP)
    table = np.einsum("sax,pq->sapqx", parts, eye)
    return split_np(table.reshape(2 * SIDE * GROUP, GROUP * NGRID))


def dot32(left, right):
    return lax.dot_general(
        left, right, (((1,), (0,)), ((), ())), preferred_element_type=jnp.float32
    )


def split(value):
    high = value.astype(jnp.bfloat16)
    low = (value - high.astype(jnp.float32)).astype(jnp.bfloat16)
    return high, low


def decode(code):
    code = code.astype(jnp.int32)
    size = jnp.abs(code) - 1
    scale = jnp.exp2((jnp.right_shift(size, 7) - 133).astype(jnp.float32))
    value = (jnp.bitwise_and(size, 127) + 128).astype(jnp.float32) * scale
    return jnp.where(code == 0, 0.0, jnp.where(code < 0, -value, value))


def add_planes(v_ref, c0_ref, c1_ref, eh_ref, el_ref, oh_ref, ol_ref, value_ref, plane_ref):
    planes = value_ref.shape[0]
    value_ref[...] = decode(v_ref[...]).reshape(value_ref.shape)
    ccount = c0_ref.shape[0]
    vcount = PAIRS // ccount
    group = 4
    lines = CHUNK // 128
    rows = group * planes
    halves = [
        [
            jnp.concatenate(
                [value_ref[:, (2 * v + half) * lines + r, :] for r in range(lines)], axis=1
            )[None]
            for half in range(2)
        ]
        for v in range(vcount)
    ]
    for c in range(0, ccount, group):
        c0 = c0_ref[c : c + group].astype(jnp.float32)
        c1 = c1_ref[c : c + group].astype(jnp.float32)
        for v in range(vcount):
            d0, d1 = halves[v][0] * c0, halves[v][1] * c1
            at = (v * ccount + c) * planes
            for which, value in enumerate((d0 + d1, d0 - d1)):
                high, low = split(value.reshape(rows, CHUNK))
                th = (eh_ref, oh_ref)[which][...]
                tl = (el_ref, ol_ref)[which][...]
                both = dot32(jnp.concatenate([high, low]), th)
                part = both[:rows] + both[rows:] + dot32(high, tl)
                plane_ref[at : at + rows, which * 256 : which * 256 + 256] += part


def finish_pairs(
    plane_ref, th_ref, tl_ref, index_ref, valence_ref, conduction_ref,
    cols_ref, rows_ref, step_ref, fold_ref, coef_ref,
):
    th, tl = th_ref[...], tl_ref[...]
    used = SIDE * GROUP
    groups = PAIRS // GROUP
    for group in range(groups):
        depth = GROUP * NGRID
        high, low = split(plane_ref[group * depth : (group + 1) * depth])
        both = dot32(th, high) + dot32(th, low) + dot32(tl, high)
        cosine, sine = both[:used], both[used:]
        for par in range(2):
            at = par * 256
            real = cosine[:, at : at + 128] + sine[:, at + 128 : at + 256]
            imag = cosine[:, at + 128 : at + 256] - sine[:, at : at + 128]
            for part, value in enumerate((real, imag)):
                first = (part * groups + group) * ROWS
                value = jnp.concatenate([value, jnp.zeros((ROWS - used, 128), jnp.float32)])
                high_part, low_part = split(value)
                fold_ref[first : first + ROWS, par * 128 : par * 128 + 128] = high_part
                fold_ref[first : first + ROWS, 256 + par * 128 : 384 + par * 128] = low_part
    width = 512
    gain = pair_gain(valence_ref, conduction_ref, conduction_ref.shape[0])

    def pick(tile, largest):
        cols = pl.ds(pl.multiple_of(tile * width, width), width)
        lane, freq, sign = sphere_slots(index_ref[:, cols])
        onehot = lax.broadcasted_iota(jnp.int32, (256, width), 0) == lane
        onehot = onehot.astype(jnp.float32).astype(jnp.bfloat16)
        picked = dot32(fold_ref[...], jnp.concatenate([onehot, onehot]))
        totals = [jnp.zeros((GROUP, width), jnp.float32)] * (2 * groups)
        for a in range(SIDE):
            here = freq == a
            for at in range(2 * groups):
                first = at * ROWS + a * GROUP
                totals[at] = jnp.where(here, picked[first : first + GROUP], totals[at])
        for part in range(2):
            total = jnp.concatenate(totals[part * groups : (part + 1) * groups]) * gain
            if part == 1:
                total = total * sign
            coef_ref[part * PAIRS : (part + 1) * PAIRS, cols] = total
            largest = jnp.maximum(largest, jnp.max(jnp.abs(total), axis=1, keepdims=True))
        return largest

    largest = lax.fori_loop(0, NG // width, pick, jnp.zeros((PAIRS, 1), jnp.float32))
    usable = largest > 1e-30
    step = jnp.ceil(jnp.log(jnp.where(usable, largest, 1.0) * (1.0 / CODES)) * (1.0 / LOG2))
    lane = lax.broadcasted_iota(jnp.int32, step_ref.shape, 1)
    powers = jnp.where(lane % 2 == 0, step, jnp.concatenate([step[8:], step[:8]]))
    step_ref[...] = powers.astype(jnp.int32).astype(jnp.int16)
    inverse = jnp.where(usable, jnp.exp2(-step), 0.0)
    inverse = jnp.concatenate([inverse, inverse])
    for block in range(32):
        codes = jnp.round(coef_ref[:, block * 128 : (block + 1) * 128] * inverse)
        codes = jnp.clip(codes, -CODES, CODES).astype(jnp.int32).astype(jnp.int16)
        rows_ref[block] = codes
        for half in range(2):
            at = half * 4 + block // 8
            cols_ref[at, :, block % 8 * 128 : block % 8 * 128 + 128] = codes


def coefficient_kernel(*refs):
    streamed, constant = refs[:7], refs[7:12]
    outputs = refs[12:15]
    value_ref, plane_ref, fold_ref, coef_ref = refs[15:]

    @pl.when(pl.program_id(0) == 0)
    def _():
        plane_ref[...] = jnp.zeros_like(plane_ref)

    add_planes(*streamed, value_ref, plane_ref)

    @pl.when(pl.program_id(0) == pl.num_programs(0) - 1)
    def _():
        finish_pairs(plane_ref, *constant, *outputs, fold_ref, coef_ref)


def pair_coefficients(valence, conduction, plane_part, line_part, index, energies):
    owners, steps, mine, lines, _ = valence.shape
    planes = owners * mine
    ccount = conduction.shape[0]
    rows = PAIRS * planes
    vspec = pl.BlockSpec((owners, 1, mine, lines, 128), lambda k: (0, k, 0, 0, 0))
    cspec = lambda off: pl.BlockSpec((ccount, planes, CHUNK), lambda k: (0, 0, k + off))
    tspec = pl.BlockSpec((CHUNK, 256), lambda k: (k, 0))
    whole = lambda shape: pl.BlockSpec(shape, lambda k: (0,) * len(shape))
    constant = [*line_part, index.reshape(1, -1)]
    scalar = pl.BlockSpec(memory_space=pltpu.SMEM)
    shapes = ((8, 2 * PAIRS, NG // 4), (32, 2 * PAIRS, NG // 32), (PAIRS, 128))
    kinds = (jnp.int16, jnp.int16, jnp.int16)
    return pl.pallas_call(
        coefficient_kernel,
        grid=(steps,),
        in_specs=[vspec, cspec(0), cspec(steps)]
        + [tspec] * 4
        + [whole(value.shape) for value in constant]
        + [scalar, scalar],
        out_specs=tuple(whole(shape) for shape in shapes),
        out_shape=tuple(jax.ShapeDtypeStruct(*both) for both in zip(shapes, kinds)),
        scratch_shapes=[
            pltpu.VMEM((planes, lines, 128), jnp.float32),
            pltpu.VMEM((rows, 512), jnp.float32),
            pltpu.VMEM((2 * (PAIRS // GROUP) * ROWS, 512), jnp.bfloat16),
            pltpu.VMEM((2 * PAIRS, NG), jnp.float32),
        ],
        compiler_params=pltpu.CompilerParams(vmem_limit_bytes=56 * 2**20),
        cost_estimate=pl.CostEstimate(
            flops=rows * FOLD * 512 * 6, bytes_accessed=40 * 2**20, transcendentals=0
        ),
        name="pair_coefficients",
    )(valence, conduction, conduction, *plane_part, *constant, *energies)


def pair_kernel(cols_ref, rows_ref, real_ref, imag_ref, total_ref):
    step = pl.program_id(0)
    values, lines, heights, height, rows = rows_ref.shape
    pieces = []
    for y in range(lines):
        for h in range(heights):
            for v in range(values):
                block = rows_ref[v, y, h].astype(jnp.float32)
                scale = -jnp.exp2(2.0 * block[2 * PAIRS :])
                block = jnp.concatenate(
                    [block[at * 8 : at * 8 + 8] * scale[:, at : at + 1] for at in range(4)]
                )
                turned = jnp.concatenate([block[PAIRS:], -block[:PAIRS]])
                pieces.append(jnp.concatenate([block, turned], axis=1))
    high, low = split(jnp.concatenate(pieces).T)
    both = jnp.concatenate([high, low])
    ch, cl = split(cols_ref[...].astype(jnp.float32))
    part = dot32(both, ch)
    part = part[: 2 * rows] + part[2 * rows :] + dot32(high, cl)

    @pl.when(step == 0)
    def _():
        total_ref[...] = part

    @pl.when(step > 0)
    def _():
        total_ref[...] += part

    @pl.when(step == pl.num_programs(0) - 1)
    def _():
        real_ref[...] = total_ref[:rows]
        imag_ref[...] = total_ref[rows:]


def pair_product(cols, rows):
    count, width = cols.shape
    values, lines, heights, height, short = rows.shape
    each = 4
    depth = count // lines * each
    shape = jax.ShapeDtypeStruct((short, width), jnp.float32)
    out = pl.BlockSpec((short, width), lambda k: (0, 0))
    return pl.pallas_call(
        pair_kernel,
        grid=(lines // each,),
        in_specs=[
            pl.BlockSpec((depth, width), lambda k: (k, 0)),
            pl.BlockSpec((values, each, heights, height, short), lambda k: (0, k, 0, 0, 0)),
        ],
        out_specs=(out, out),
        out_shape=(shape, shape),
        scratch_shapes=[pltpu.VMEM((2 * short, width), jnp.float32)],
        compiler_params=pltpu.CompilerParams(vmem_limit_bytes=48 * 2**20),
        cost_estimate=pl.CostEstimate(
            flops=6 * 2 * short * width * count, bytes_accessed=12 * 2**20, transcendentals=0
        ),
        name="pair_product",
    )(cols, rows)


def sphere_slots(index):
    def quotient(value, divisor):
        exact = (value.astype(jnp.float32) + 0.5) * (1.0 / divisor)
        return jnp.floor(exact).astype(jnp.int32)

    def folded(value):
        return jnp.where(value >= HALF, value - NGRID, value)

    first = quotient(index, PLANE)
    rest = index - first * PLANE
    second = quotient(rest, NGRID)
    third = folded(rest - second * NGRID)
    first, second = folded(first), folded(second)
    sign = jnp.where(third < 0, -1, 1)
    first, second, third = first * sign, second * sign, third * sign
    turn = second + KCUT
    lane = jnp.right_shift(turn, 1) * ELEN + third + jnp.bitwise_and(turn, 1) * 128
    return lane, first + KCUT, sign.astype(jnp.float32)


def pair_gain(valence_ref, conduction_ref, ccount):
    at = lax.broadcasted_iota(jnp.int32, (PAIRS, 1), 0)
    gap = jnp.zeros((PAIRS, 1), jnp.float32)
    for pair in range(PAIRS):
        this = conduction_ref[pair % ccount] - valence_ref[pair // ccount]
        gap = jnp.where(at == pair, this, gap)
    return jnp.sqrt(2.0 / gap * 2048.0**-0.5) * float(NGRID) ** -1.5


def encode(values):
    size = jnp.abs(values.astype(jnp.float32))
    tiny = size < 2.0**-126
    size = jnp.where(tiny, 1.0, size)
    power = jnp.floor(jnp.log2(size))
    code = (power + 126.0) * 128.0 + jnp.round((size * jnp.exp2(-power) - 1.0) * 128.0) + 1.0
    return jnp.where(tiny, 0.0, jnp.where(values < 0, -code, code)).astype(jnp.int16)


def gather_planes(orbitals):
    count, mine = orbitals.shape[:2]
    lines = CHUNK // 128
    steps = FOLD // CHUNK
    codes = encode(orbitals).reshape(count, mine, 2, steps, lines, 128)
    codes = jnp.transpose(codes, (3, 1, 0, 2, 4, 5)).reshape(-1, 128)
    codes = lax.all_gather(codes, "zh", axis=0)
    codes = lax.all_gather(codes, ("y", "x"), axis=0)
    return codes.reshape(32, steps, mine, 2 * count * lines, 128)


def columns_and_rows(cols, rows, steps):
    height, short = rows.shape[1:]
    sent = jnp.concatenate(
        [
            jnp.broadcast_to(rows, (4,) + rows.shape),
            jnp.broadcast_to(steps[:8], (4, 32, 8, short)),
        ],
        axis=2,
    ).reshape(128, height + 8, short)
    sent = lax.all_to_all(sent, VAL + COND, 0, 0, tiled=True)
    line = lax.all_to_all(cols, ("zh",) + VAL, 0, 0, tiled=True)
    cols = lax.all_gather(line, ("y", "x"), axis=0).reshape(-1, cols.shape[-1])
    return cols, sent.reshape(4, 16, 2, height + 8, short)


def per_device(
    valence_orbitals, conduction_orbitals, valence_energy, conduction_energy, sphere_index
):
    coded = pair_coefficients(
        gather_planes(valence_orbitals),
        conduction_orbitals,
        plane_tables(),
        line_tables(),
        sphere_index,
        (valence_energy, conduction_energy),
    )
    return pair_product(*columns_and_rows(*coded))


def solution(mesh):
    names = ("zl", "core", "y", "x", "zh")
    fine = Mesh(mesh.devices.reshape(2, 2, 4, 4, 2), names)
    placed = (P(VAL, COND, None), P(COND, None, None), P(VAL), P(COND), P())
    return jax.shard_map(
        per_device,
        mesh=fine,
        in_specs=placed,
        out_specs=(P(COND, VAL), P(COND, VAL)),
        check_vma=False,
    )
```

time: 207 us -> 186 us (0.90)
  local copies, waits for them, and re-layouts: 16.5 us -> 1.93 us
  other arithmetic: 7.34 us -> 3.14 us
  waiting for transfers between devices: 10.2 us -> 7.2 us
    reshape x2, local copies, waits for them, and re-layouts: 6.43 us -> 0.12 us  [gather_planes(): codes = encode(orbitals).reshape(count, mine, 2, steps, lines, 128)]
    all_to_all x2, waiting for transfers between devices: 10.2 us -> 7.2 us  [the longest x1 7.2 us: columns_and_rows(): line = lax.all_to_all(cols, ('zh',) + VAL, 0, 0, tiled=True)]
    transpose x1 -> x0, local copies, waits for them, and re-layouts: 2.42 us -> none  [gather_planes(): return jnp.swapaxes(values, 0, 1).reshape(count, NGRID, PLANE)]
    neg x2 -> x0, local copies, waits for them, and re-layouts: 2.22 us -> none  [rows_of_all(): return (got[..., :height, :].reshape(-1, rows), -scale)]
    pallas_call x3 -> x2, Pallas kernels: 55.1 us -> 56.9 us  [the longest x1 45.2 us: pair_coefficients(): pl.pallas_call(coefficient_kernel, grid=(steps,), in_specs=[vspec, cspec(...]
  transfers between devices with their start and end apart: 2 -> 2, of which waited for: 1 -> 1; matrix products, arithmetic and copies ran while one was open for 0% -> 2% of each run, Pallas kernels for 0% -> 0%
where the time goes in v2:
time: 186 us
  blocking collectives  106 us (57%)
  Pallas kernels  56.9 us (31%)
  starting transfers between devices  10.1 us (5%)
  waiting for transfers between devices  7.2 us (4%)
  other arithmetic  3.14 us (2%)
  local copies, waits for them, and re-layouts  1.93 us (1%)
    all_gather x1, blocking collectives, columns_and_rows(): cols = lax.all_gather(line, ('y', 'x'), axis=0).reshape(-1, cols.shape[-1])  64.3 us
    pallas_call x1, Pallas kernels, pair_coefficients(): pl.pallas_call(coefficient_kernel, grid=(steps,), in_specs=[vspec, cspec(...  45.2 us
    all_gather x1, blocking collectives, gather_planes(): codes = lax.all_gather(codes, ('y', 'x'), axis=0)  33.9 us
    pallas_call x1, Pallas kernels, pair_product(): pl.pallas_call(pair_kernel, grid=(lines // each,), in_specs=[pl.BlockSpec...  11.6 us
    all_gather x1, blocking collectives, gather_planes(): codes = lax.all_gather(codes, 'zh', axis=0)  7.67 us
    all_to_all x1, waiting for transfers between devices, columns_and_rows(): line = lax.all_to_all(cols, ('zh',) + VAL, 0, 0, tiled=True)  7.2 us
    all_to_all x1, starting transfers between devices, columns_and_rows(): sent = lax.all_to_all(sent, VAL + COND, 0, 0, tiled=True)  5.49 us
    all_to_all x1, starting transfers between devices, columns_and_rows(): line = lax.all_to_all(cols, ('zh',) + VAL, 0, 0, tiled=True)  4.56 us
  transfers between devices with their start and end apart: 2, of which 1 were waited for; matrix products, arithmetic and copies ran while one was open for 2% of the time, Pallas kernels for 0%

profile of v2, /device:TPU:0, one launch (start us, length us, event | category | flops | bytes accessed | tf_op | source)
XLA Modules:
  0.0 185.8 jit_solution(6309056071108902818)
XLA Ops:
  0.6 1.8 fusion
  2.4 0.1 reshape.22
  2.6 7.7 %all_gather.15 = s16[2,432,128]{2,1,0:T(8,128)(2,1)S(1)} all-gather(s16[1,432,128]{2,1,0:T(8,128)(2,1)S(1)} %bitcast.13), channel_id=1, replica_groups=mesh['zl'=2,'core'=2,'y'=4,'x'=4,'zh'=2] {'zh'}, dimensions={0}, use_global_device_ids=true | all-gather | bytes 331776 | tf_op jit(solution)/shard_map/all_gather | solution.py:331
  10.2 33.9 %all-gather.4 = s16[32,432,128]{2,1,0:T(8,128)(2,1)} all-gather(s16[2,432,128]{2,1,0:T(8,128)(2,1)S(1)} %all_gather.15), channel_id=2, replica_groups=mesh['zl'=2,'core'=2,'y'=4,'x'=4,'zh'=2] {'y','x'}, dimensions={0}, use_global_device_ids=true | all-gather | bytes 3760128 | tf_op jit(solution)/shard_map/all_gather | solution.py:332
  44.2 45.2 %pair_coefficients.1 = (s16[8,32,1024]{2,1,0:T(8,128)(2,1)}, s16[32,32,128]{2,1,0:T(8,128)(2,1)}, s16[16,128]{1,0:T(8,128)(2,1)}) custom-call(s16[32,9,3,16,128]{4,3,2,1,0:T(8,128)(2,1)} %bitcast.12, bf16[8,96,9216]{2,1,0:T(8,128)(2,1)} %refs_2_.1, bf16[8,96,9216]{2,1,0:T(8,128)(2,1)} %refs_2_.1, bf16[4608,256]{1,0:T(8,128)(2,1)} %constant.31.clone.refs_3_, ...), custom_call_target="tpu_custom_call" | custom-call | flops 21743271936 | bytes 41943040 | tf_op jit(solution)/shard_map/pair_coefficients/pallas_call | solution.py:205
  89.4 4.6 %all-to-all-start = ((s16[8,32,1024]{2,1,0:T(8,128)(2,1)}), s16[8,32,1024]{2,1,0:T(8,128)(2,1)S(1)}, u32[]{:S(2)}, u32[]{:S(2)}) async-start(s16[8,32,1024]{2,1,0:T(8,128)(2,1)} %get-tuple-element.5), calls=%async_computation | async-start | bytes 1048576 | tf_op jit(solution)/shard_map/all_to_all | solution.py:346
  94.0 0.7 slice.3
  94.7 1.1 broadcast_in_dim.15
  95.8 1.3 pad_add_fusion
  97.1 7.2 %all-to-all-done = s16[8,32,1024]{2,1,0:T(8,128)(2,1)S(1)} async-done(((s16[8,32,1024]{2,1,0:T(8,128)(2,1)}), s16[8,32,1024]{2,1,0:T(8,128)(2,1)S(1)}, u32[]{:S(2)}, u32[]{:S(2)}) %all-to-all-start) | async-done | bytes 524320 | tf_op jit(solution)/shard_map/all_to_all | solution.py:346
  104.3 5.5 %all-to-all-start.1 = ((s16[128,40,128]{2,1,0:T(8,128)(2,1)}), s16[128,40,128]{2,1,0:T(8,128)(2,1)S(1)}, u32[]{:S(2)}, u32[]{:S(2)}) async-start(s16[128,40,128]{2,1,0:T(8,128)(2,1)} %bitcast.5), calls=%async_computation.1 | async-start | bytes 2621440 | tf_op jit(solution)/shard_map/all_to_all | solution.py:345
  109.8 64.3 %all-gather.5 = s16[128,32,1024]{2,1,0:T(8,128)(2,1)} all-gather(s16[8,32,1024]{2,1,0:T(8,128)(2,1)S(1)} %all-to-all-done), channel_id=3, replica_groups=mesh['zl'=2,'core'=2,'y'=4,'x'=4,'zh'=2] {'y','x'}, dimensions={0}, use_global_device_ids=true | all-gather | bytes 8912896 | tf_op jit(solution)/shard_map/all_gather | solution.py:347
  174.2 0.0 all-to-all-done.1
  174.2 11.6 %pair_product.1 = (f32[128,1024]{1,0:T(8,128)}, f32[128,1024]{1,0:T(8,128)}) custom-call(s16[4096,1024]{1,0:T(8,128)(2,1)} %bitcast.11, s16[4,16,2,40,128]{4,3,2,1,0:T(8,128)(2,1)S(1)} %bitcast.10), custom_call_target="tpu_custom_call" | custom-call | flops 6442450944 | bytes 12582912 | tf_op jit(solution)/shard_map/pair_product/pallas_call | solution.py:269
  (2 shorter events, 0.1 us)
Async XLA Ops:
  89.4 14.9 %all-to-all-start = ((s16[8,32,1024]{2,1,0:T(8,128)(2,1)}), s16[8,32,1024]{2,1,0:T(8,128)(2,1)S(1)}, u32[]{:S(2)}, u32[]{:S(2)}) async-start(s16[8,32,1024]{2,1,0:T(8,128)(2,1)} %get-tuple-element.5), calls=%async_computation | async-start | bytes 1048576 | tf_op jit(solution)/shard_map/all_to_all | solution.py:346
  104.3 69.9 %all-to-all-start.1 = ((s16[128,40,128]{2,1,0:T(8,128)(2,1)}), s16[128,40,128]{2,1,0:T(8,128)(2,1)S(1)}, u32[]{:S(2)}, u32[]{:S(2)}) async-start(s16[128,40,128]{2,1,0:T(8,128)(2,1)} %bitcast.5), calls=%async_computation.1 | async-start | bytes 2621440 | tf_op jit(solution)/shard_map/all_to_all | solution.py:345

commit v3 on v2

--- a/solution.py
+++ b/solution.py
@@ -73,41 +73,42 @@
 
 def decode(code):
     code = code.astype(jnp.int32)
-    size = jnp.abs(code) - 1
-    scale = jnp.exp2((jnp.right_shift(size, 7) - 133).astype(jnp.float32))
-    value = (jnp.bitwise_and(size, 127) + 128).astype(jnp.float32) * scale
-    return jnp.where(code == 0, 0.0, jnp.where(code < 0, -value, value))
+    scale = jnp.exp2(jnp.right_shift(code, 8).astype(jnp.float32))
+    low = jnp.bitwise_and(code, 255).astype(jnp.float32)
+    return jnp.where(low < 128.0, low + 128.0, -low) * scale
 
 
 def add_planes(v_ref, c0_ref, c1_ref, eh_ref, el_ref, oh_ref, ol_ref, value_ref, plane_ref):
-    planes = value_ref.shape[0]
-    value_ref[...] = decode(v_ref[...]).reshape(value_ref.shape)
+    vcount, each, planes = value_ref.shape[:3]
+    values = decode(v_ref[...]).reshape(planes, vcount * each, 128)
+    for v in range(vcount):
+        value_ref[v] = jnp.swapaxes(values[:, v * each : (v + 1) * each], 0, 1)
     ccount = c0_ref.shape[0]
-    vcount = PAIRS // ccount
-    group = 4
+    group, each = 4, 16
     lines = CHUNK // 128
     rows = group * planes
-    halves = [
-        [
-            jnp.concatenate(
-                [value_ref[:, (2 * v + half) * lines + r, :] for r in range(lines)], axis=1
-            )[None]
-            for half in range(2)
-        ]
-        for v in range(vcount)
-    ]
     for c in range(0, ccount, group):
-        c0 = c0_ref[c : c + group].astype(jnp.float32)
-        c1 = c1_ref[c : c + group].astype(jnp.float32)
         for v in range(vcount):
-            d0, d1 = halves[v][0] * c0, halves[v][1] * c1
+            parts = [[], []], [[], []]
+            for band in range(c, c + group):
+                for first in range(0, planes, each):
+                    here = slice(first, first + each)
+                    d0, d1 = (
+                        jnp.concatenate(
+                            [value_ref[v, half * lines + r, here] for r in range(lines)], axis=1
+                        )
+                        * c_ref[band, here].astype(jnp.float32)
+                        for half, c_ref in enumerate((c0_ref, c1_ref))
+                    )
+                    for which, value in enumerate((d0 + d1, d0 - d1)):
+                        for part, value in zip(parts[which], split(value)):
+                            part.append(value)
             at = (v * ccount + c) * planes
-            for which, value in enumerate((d0 + d1, d0 - d1)):
-                high, low = split(value.reshape(rows, CHUNK))
+            for which, (highs, lows) in enumerate(parts):
                 th = (eh_ref, oh_ref)[which][...]
                 tl = (el_ref, ol_ref)[which][...]
-                both = dot32(jnp.concatenate([high, low]), th)
-                part = both[:rows] + both[rows:] + dot32(high, tl)
+                both = dot32(jnp.concatenate(highs + lows), th)
+                part = both[:rows] + both[rows:] + dot32(jnp.concatenate(highs), tl)
                 plane_ref[at : at + rows, which * 256 : which * 256 + 256] += part
 
 
@@ -137,7 +138,7 @@
     gain = pair_gain(valence_ref, conduction_ref, conduction_ref.shape[0])
 
     def pick(tile, largest):
-        cols = pl.ds(pl.multiple_of(tile * width, width), width)
+        cols = slice(tile * width, (tile + 1) * width)
         lane, freq, sign = sphere_slots(index_ref[:, cols])
         onehot = lax.broadcasted_iota(jnp.int32, (256, width), 0) == lane
         onehot = onehot.astype(jnp.float32).astype(jnp.bfloat16)
@@ -156,7 +157,9 @@
             largest = jnp.maximum(largest, jnp.max(jnp.abs(total), axis=1, keepdims=True))
         return largest
 
-    largest = lax.fori_loop(0, NG // width, pick, jnp.zeros((PAIRS, 1), jnp.float32))
+    largest = jnp.zeros((PAIRS, 1), jnp.float32)
+    for tile in range(NG // width):
+        largest = pick(tile, largest)
     usable = largest > 1e-30
     step = jnp.ceil(jnp.log(jnp.where(usable, largest, 1.0) * (1.0 / CODES)) * (1.0 / LOG2))
     lane = lax.broadcasted_iota(jnp.int32, step_ref.shape, 1)
@@ -212,7 +215,7 @@
         out_specs=tuple(whole(shape) for shape in shapes),
         out_shape=tuple(jax.ShapeDtypeStruct(*both) for both in zip(shapes, kinds)),
         scratch_shapes=[
-            pltpu.VMEM((planes, lines, 128), jnp.float32),
+            pltpu.VMEM((PAIRS // ccount, 2 * CHUNK // 128, planes, 128), jnp.float32),
             pltpu.VMEM((rows, 512), jnp.float32),
             pltpu.VMEM((2 * (PAIRS // GROUP) * ROWS, 512), jnp.bfloat16),
             pltpu.VMEM((2 * PAIRS, NG), jnp.float32),
@@ -315,11 +318,14 @@
 
 def encode(values):
     size = jnp.abs(values.astype(jnp.float32))
-    tiny = size < 2.0**-126
+    tiny = size < 2.0**-120
     size = jnp.where(tiny, 1.0, size)
     power = jnp.floor(jnp.log2(size))
-    code = (power + 126.0) * 128.0 + jnp.round((size * jnp.exp2(-power) - 1.0) * 128.0) + 1.0
-    return jnp.where(tiny, 0.0, jnp.where(values < 0, -code, code)).astype(jnp.int16)
+    mantissa = jnp.round(size * jnp.exp2(7.0 - power)) - 128.0
+    power = jnp.where(mantissa > 127.0, power + 1.0, power) - 7.0
+    mantissa = jnp.where(mantissa > 127.0, 0.0, mantissa)
+    code = power * 256.0 + mantissa + jnp.where(values < 0, 128.0, 0.0)
+    return jnp.where(tiny, -32768.0, code).astype(jnp.int16)
 
 
 def gather_planes(orbitals):

time: 186 us -> 177 us (0.952)
  Pallas kernels: 56.9 us -> 47.9 us
    pallas_call x1, Pallas kernels: 45.2 us -> 36.2 us  [pair_coefficients(): pl.pallas_call(coefficient_kernel, grid=(steps,), in_specs=[vspec, cspec(...]
where the time goes in v3:
time: 177 us
  blocking collectives  106 us (60%)
  Pallas kernels  47.9 us (27%)
  starting transfers between devices  10.2 us (6%)
  waiting for transfers between devices  7.2 us (4%)
  other arithmetic  3.22 us (2%)
  local copies, waits for them, and re-layouts  1.93 us (1%)
    all_gather x1, blocking collectives, columns_and_rows(): cols = lax.all_gather(line, ('y', 'x'), axis=0).reshape(-1, cols.shape[-1])  64.3 us
    pallas_call x1, Pallas kernels, pair_coefficients(): pl.pallas_call(coefficient_kernel, grid=(steps,), in_specs=[vspec, cspec(...  36.2 us
    all_gather x1, blocking collectives, gather_planes(): codes = lax.all_gather(codes, ('y', 'x'), axis=0)  33.9 us
    pallas_call x1, Pallas kernels, pair_product(): pl.pallas_call(pair_kernel, grid=(lines // each,), in_specs=[pl.BlockSpec...  11.6 us
    all_gather x1, blocking collectives, gather_planes(): codes = lax.all_gather(codes, 'zh', axis=0)  7.67 us
    all_to_all x1, waiting for transfers between devices, columns_and_rows(): line = lax.all_to_all(cols, ('zh',) + VAL, 0, 0, tiled=True)  7.2 us
    all_to_all x1, starting transfers between devices, columns_and_rows(): sent = lax.all_to_all(sent, VAL + COND, 0, 0, tiled=True)  5.62 us
    all_to_all x1, starting transfers between devices, columns_and_rows(): line = lax.all_to_all(cols, ('zh',) + VAL, 0, 0, tiled=True)  4.55 us
  transfers between devices with their start and end apart: 2, of which 1 were waited for; matrix products, arithmetic and copies ran while one was open for 2% of the time, Pallas kernels for 0%

profile of v3, /device:TPU:0, one launch (start us, length us, event | category | flops | bytes accessed | tf_op | source)
XLA Modules:
  0.0 177.0 jit_solution(17695178818513783441)
XLA Ops:
  0.6 1.9 %fusion.4 = s16[2,3,9216]{2,0,1:T(2,128)(2,1)S(1)} fusion(bf16[2,3,9216]{2,0,1:T(2,128)(2,1)} %param.11), kind=kLoop, calls=%fused_computation.10 | loop fusion | flops 1382400 | bytes 221184 | tf_op jit(solution)/shard_map/convert_element_type | solution.py:328
  2.5 0.1 reshape.22
  2.7 7.7 %all_gather.15 = s16[2,432,128]{2,1,0:T(8,128)(2,1)S(1)} all-gather(s16[1,432,128]{2,1,0:T(8,128)(2,1)S(1)} %bitcast.13), channel_id=1, replica_groups=mesh['zl'=2,'core'=2,'y'=4,'x'=4,'zh'=2] {'zh'}, dimensions={0}, use_global_device_ids=true | all-gather | bytes 331776 | tf_op jit(solution)/shard_map/all_gather | solution.py:337
  10.3 33.9 %all-gather.4 = s16[32,432,128]{2,1,0:T(8,128)(2,1)} all-gather(s16[2,432,128]{2,1,0:T(8,128)(2,1)S(1)} %all_gather.15), channel_id=2, replica_groups=mesh['zl'=2,'core'=2,'y'=4,'x'=4,'zh'=2] {'y','x'}, dimensions={0}, use_global_device_ids=true | all-gather | bytes 3760128 | tf_op jit(solution)/shard_map/all_gather | solution.py:338
  44.3 36.2 %pair_coefficients.1 = (s16[8,32,1024]{2,1,0:T(8,128)(2,1)}, s16[32,32,128]{2,1,0:T(8,128)(2,1)}, s16[16,128]{1,0:T(8,128)(2,1)}) custom-call(s16[32,9,3,16,128]{4,3,2,1,0:T(8,128)(2,1)} %bitcast.12, bf16[8,96,9216]{2,1,0:T(8,128)(2,1)} %refs_2_.1, bf16[8,96,9216]{2,1,0:T(8,128)(2,1)} %refs_2_.1, bf16[4608,256]{1,0:T(8,128)(2,1)} %constant.40.clone.refs_3_, ...), custom_call_target="tpu_custom_call" | custom-call | flops 21743271936 | bytes 41943040 | tf_op jit(solution)/shard_map/pair_coefficients/pallas_call | solution.py:208
  80.5 4.5 %all-to-all-start = ((s16[8,32,1024]{2,1,0:T(8,128)(2,1)}), s16[8,32,1024]{2,1,0:T(8,128)(2,1)S(1)}, u32[]{:S(2)}, u32[]{:S(2)}) async-start(s16[8,32,1024]{2,1,0:T(8,128)(2,1)} %get-tuple-element.5), calls=%async_computation | async-start | bytes 1048576 | tf_op jit(solution)/shard_map/all_to_all | solution.py:352
  85.1 0.7 slice.3
  85.8 1.1 broadcast_in_dim.23
  86.9 1.3 pad_add_fusion
  88.2 7.2 %all-to-all-done = s16[8,32,1024]{2,1,0:T(8,128)(2,1)S(1)} async-done(((s16[8,32,1024]{2,1,0:T(8,128)(2,1)}), s16[8,32,1024]{2,1,0:T(8,128)(2,1)S(1)}, u32[]{:S(2)}, u32[]{:S(2)}) %all-to-all-start) | async-done | bytes 524320 | tf_op jit(solution)/shard_map/all_to_all | solution.py:352
  95.4 5.6 %all-to-all-start.1 = ((s16[128,40,128]{2,1,0:T(8,128)(2,1)}), s16[128,40,128]{2,1,0:T(8,128)(2,1)S(1)}, u32[]{:S(2)}, u32[]{:S(2)}) async-start(s16[128,40,128]{2,1,0:T(8,128)(2,1)} %bitcast.5), calls=%async_computation.1 | async-start | bytes 2621440 | tf_op jit(solution)/shard_map/all_to_all | solution.py:351
  101.0 64.3 %all-gather.5 = s16[128,32,1024]{2,1,0:T(8,128)(2,1)} all-gather(s16[8,32,1024]{2,1,0:T(8,128)(2,1)S(1)} %all-to-all-done), channel_id=3, replica_groups=mesh['zl'=2,'core'=2,'y'=4,'x'=4,'zh'=2] {'y','x'}, dimensions={0}, use_global_device_ids=true | all-gather | bytes 8912896 | tf_op jit(solution)/shard_map/all_gather | solution.py:353
  165.4 0.0 all-to-all-done.1
  165.4 11.6 %pair_product.1 = (f32[128,1024]{1,0:T(8,128)}, f32[128,1024]{1,0:T(8,128)}) custom-call(s16[4096,1024]{1,0:T(8,128)(2,1)} %bitcast.11, s16[4,16,2,40,128]{4,3,2,1,0:T(8,128)(2,1)S(1)} %bitcast.10), custom_call_target="tpu_custom_call" | custom-call | flops 6442450944 | bytes 12582912 | tf_op jit(solution)/shard_map/pair_product/pallas_call | solution.py:272
  (2 shorter events, 0.1 us)
Async XLA Ops:
  80.5 14.9 %all-to-all-start = ((s16[8,32,1024]{2,1,0:T(8,128)(2,1)}), s16[8,32,1024]{2,1,0:T(8,128)(2,1)S(1)}, u32[]{:S(2)}, u32[]{:S(2)}) async-start(s16[8,32,1024]{2,1,0:T(8,128)(2,1)} %get-tuple-element.5), calls=%async_computation | async-start | bytes 1048576 | tf_op jit(solution)/shard_map/all_to_all | solution.py:352
  95.4 70.0 %all-to-all-start.1 = ((s16[128,40,128]{2,1,0:T(8,128)(2,1)}), s16[128,40,128]{2,1,0:T(8,128)(2,1)S(1)}, u32[]{:S(2)}, u32[]{:S(2)}) async-start(s16[128,40,128]{2,1,0:T(8,128)(2,1)} %bitcast.5), calls=%async_computation.1 | async-start | bytes 2621440 | tf_op jit(solution)/shard_map/all_to_all | solution.py:351

commit v4 on v3

--- a/solution.py
+++ b/solution.py
@@ -114,7 +114,7 @@
 
 def finish_pairs(
     plane_ref, th_ref, tl_ref, index_ref, valence_ref, conduction_ref,
-    cols_ref, rows_ref, step_ref, fold_ref, coef_ref,
+    cols_ref, rows_ref, fold_ref, coef_ref,
 ):
     th, tl = th_ref[...], tl_ref[...]
     used = SIDE * GROUP
@@ -162,24 +162,28 @@
         largest = pick(tile, largest)
     usable = largest > 1e-30
     step = jnp.ceil(jnp.log(jnp.where(usable, largest, 1.0) * (1.0 / CODES)) * (1.0 / LOG2))
-    lane = lax.broadcasted_iota(jnp.int32, step_ref.shape, 1)
-    powers = jnp.where(lane % 2 == 0, step, jnp.concatenate([step[8:], step[:8]]))
-    step_ref[...] = powers.astype(jnp.int32).astype(jnp.int16)
+    lane = lax.broadcasted_iota(jnp.int32, (8, 128), 1)
+    powers = jnp.where(lane % 2 == 0, step[:8], step[8:]).astype(jnp.int32)
     inverse = jnp.where(usable, jnp.exp2(-step), 0.0)
     inverse = jnp.concatenate([inverse, inverse])
-    for block in range(32):
-        codes = jnp.round(coef_ref[:, block * 128 : (block + 1) * 128] * inverse)
-        codes = jnp.clip(codes, -CODES, CODES).astype(jnp.int32).astype(jnp.int16)
-        rows_ref[block] = codes
-        for half in range(2):
-            at = half * 4 + block // 8
-            cols_ref[at, :, block % 8 * 128 : block % 8 * 128 + 128] = codes
+    each = cols_ref.shape[0] // 2
+    for owner in range(each):
+        blocks = []
+        for block in range(owner * 8, owner * 8 + 8):
+            codes = jnp.round(coef_ref[:, block * 128 : (block + 1) * 128] * inverse)
+            codes = jnp.clip(codes, -CODES, CODES).astype(jnp.int32)
+            for copy in range(0, rows_ref.shape[0], 32):
+                rows_ref[copy + block] = codes.astype(jnp.int16)
+            blocks.append(codes)
+        message = jnp.concatenate(blocks + [powers]).astype(jnp.int16)
+        cols_ref[owner] = message
+        cols_ref[each + owner] = message
 
 
 def coefficient_kernel(*refs):
     streamed, constant = refs[:7], refs[7:12]
-    outputs = refs[12:15]
-    value_ref, plane_ref, fold_ref, coef_ref = refs[15:]
+    outputs = refs[12:14]
+    value_ref, plane_ref, fold_ref, coef_ref = refs[14:]
 
     @pl.when(pl.program_id(0) == 0)
     def _():
@@ -203,8 +207,7 @@
     whole = lambda shape: pl.BlockSpec(shape, lambda k: (0,) * len(shape))
     constant = [*line_part, index.reshape(1, -1)]
     scalar = pl.BlockSpec(memory_space=pltpu.SMEM)
-    shapes = ((8, 2 * PAIRS, NG // 4), (32, 2 * PAIRS, NG // 32), (PAIRS, 128))
-    kinds = (jnp.int16, jnp.int16, jnp.int16)
+    shapes = ((8, 8 * 2 * PAIRS + 8, 128), (128, 2 * PAIRS, 128))
     return pl.pallas_call(
         coefficient_kernel,
         grid=(steps,),
@@ -213,7 +216,7 @@
         + [whole(value.shape) for value in constant]
         + [scalar, scalar],
         out_specs=tuple(whole(shape) for shape in shapes),
-        out_shape=tuple(jax.ShapeDtypeStruct(*both) for both in zip(shapes, kinds)),
+        out_shape=tuple(jax.ShapeDtypeStruct(shape, jnp.int16) for shape in shapes),
         scratch_shapes=[
             pltpu.VMEM((PAIRS // ccount, 2 * CHUNK // 128, planes, 128), jnp.float32),
             pltpu.VMEM((rows, 512), jnp.float32),
@@ -231,20 +234,27 @@
 def pair_kernel(cols_ref, rows_ref, real_ref, imag_ref, total_ref):
     step = pl.program_id(0)
     values, lines, heights, height, rows = rows_ref.shape
-    pieces = []
+    blocks = total_ref.shape[1] // 128
+    row_pieces, col_pieces = [], []
     for y in range(lines):
         for h in range(heights):
             for v in range(values):
+                codes = cols_ref[y, h * values + v].astype(jnp.float32)
+                col_pieces.append(
+                    jnp.concatenate(
+                        [codes[at * height : (at + 1) * height] for at in range(blocks)], axis=1
+                    )
+                )
+                scale = -jnp.exp2(2.0 * codes[blocks * height :])
                 block = rows_ref[v, y, h].astype(jnp.float32)
-                scale = -jnp.exp2(2.0 * block[2 * PAIRS :])
                 block = jnp.concatenate(
-                    [block[at * 8 : at * 8 + 8] * scale[:, at : at + 1] for at in range(4)]
+                    [block[at * 8 : at * 8 + 8] * scale[:, at : at + 1] for at in range(height // 8)]
                 )
                 turned = jnp.concatenate([block[PAIRS:], -block[:PAIRS]])
-                pieces.append(jnp.concatenate([block, turned], axis=1))
-    high, low = split(jnp.concatenate(pieces).T)
+                row_pieces.append(jnp.concatenate([block, turned], axis=1))
+    high, low = split(jnp.concatenate(row_pieces).T)
     both = jnp.concatenate([high, low])
-    ch, cl = split(cols_ref[...].astype(jnp.float32))
+    ch, cl = split(jnp.concatenate(col_pieces))
     part = dot32(both, ch)
     part = part[: 2 * rows] + part[2 * rows :] + dot32(high, cl)
 
@@ -263,17 +273,17 @@
 
 
 def pair_product(cols, rows):
-    count, width = cols.shape
     values, lines, heights, height, short = rows.shape
+    width = cols.shape[2] // height * 128
+    count = lines * heights * values * height
     each = 4
-    depth = count // lines * each
     shape = jax.ShapeDtypeStruct((short, width), jnp.float32)
     out = pl.BlockSpec((short, width), lambda k: (0, 0))
     return pl.pallas_call(
         pair_kernel,
         grid=(lines // each,),
         in_specs=[
-            pl.BlockSpec((depth, width), lambda k: (k, 0)),
+            pl.BlockSpec((each,) + cols.shape[1:], lambda k: (k, 0, 0, 0)),
             pl.BlockSpec((values, each, heights, height, short), lambda k: (0, k, 0, 0, 0)),
         ],
         out_specs=(out, out),
@@ -339,19 +349,10 @@
     return codes.reshape(32, steps, mine, 2 * count * lines, 128)
 
 
-def columns_and_rows(cols, rows, steps):
-    height, short = rows.shape[1:]
-    sent = jnp.concatenate(
-        [
-            jnp.broadcast_to(rows, (4,) + rows.shape),
-            jnp.broadcast_to(steps[:8], (4, 32, 8, short)),
-        ],
-        axis=2,
-    ).reshape(128, height + 8, short)
-    sent = lax.all_to_all(sent, VAL + COND, 0, 0, tiled=True)
+def columns_and_rows(cols, rows):
+    sent = lax.all_to_all(rows, VAL + COND, 0, 0, tiled=True)
     line = lax.all_to_all(cols, ("zh",) + VAL, 0, 0, tiled=True)
-    cols = lax.all_gather(line, ("y", "x"), axis=0).reshape(-1, cols.shape[-1])
-    return cols, sent.reshape(4, 16, 2, height + 8, short)
+    return lax.all_gather(line, ("y", "x"), axis=0), sent.reshape((4, 16, 2) + rows.shape[1:])
 
 
 def per_device(

time: 177 us -> 176 us (level)
  blocking collectives: 106 us -> 119 us
  waiting for transfers between devices: 7.2 us -> 0.01 us
  starting transfers between devices: 10.2 us -> 5.67 us
  local copies, waits for them, and re-layouts: 1.93 us -> 0.12 us
    all_to_all x0 -> x1, blocking collectives: none -> 15.1 us  [columns_and_rows(): line = lax.all_to_all(cols, ('zh',) + VAL, 0, 0, tiled=True)]
    all_to_all x2 -> x1, waiting for transfers between devices: 7.2 us -> 0.01 us  [columns_and_rows(): sent = lax.all_to_all(rows, VAL + COND, 0, 0, tiled=True)]
    all_to_all x2 -> x1, starting transfers between devices: 10.2 us -> 5.67 us  [columns_and_rows(): sent = lax.all_to_all(rows, VAL + COND, 0, 0, tiled=True)]
  transfers between devices with their start and end apart: 2 -> 1, of which waited for: 1 -> 0; matrix products, arithmetic and copies ran while one was open for 2% -> 0% of each run, Pallas kernels for 0% -> 0%
where the time goes in v4:
time: 176 us
  blocking collectives  119 us (68%)
  Pallas kernels  48.3 us (27%)
  starting transfers between devices  5.67 us (3%)
  other arithmetic  1.9 us (1%)
    all_gather x1, blocking collectives, columns_and_rows(): lax.all_gather(line, ('y', 'x'), axis=0)  62.7 us
    pallas_call x1, Pallas kernels, pair_coefficients(): pl.pallas_call(coefficient_kernel, grid=(steps,), in_specs=[vspec, cspec(...  36.7 us
    all_gather x1, blocking collectives, gather_planes(): codes = lax.all_gather(codes, ('y', 'x'), axis=0)  33.9 us
    all_to_all x1, blocking collectives, columns_and_rows(): line = lax.all_to_all(cols, ('zh',) + VAL, 0, 0, tiled=True)  15.1 us
    pallas_call x1, Pallas kernels, pair_product(): pl.pallas_call(pair_kernel, grid=(lines // each,), in_specs=[pl.BlockSpec...  11.7 us
    all_gather x1, blocking collectives, gather_planes(): codes = lax.all_gather(codes, 'zh', axis=0)  7.67 us
    all_to_all x1, starting transfers between devices, columns_and_rows(): sent = lax.all_to_all(rows, VAL + COND, 0, 0, tiled=True)  5.67 us
  transfers between devices with their start and end apart: 1, of which 0 were waited for; matrix products, arithmetic and copies ran while one was open for 0% of the time, Pallas kernels for 0%

profile of v4, /device:TPU:0, one launch (start us, length us, event | category | flops | bytes accessed | tf_op | source)
XLA Modules:
  0.0 176.0 jit_solution(10146474974516878175)
XLA Ops:
  0.6 1.9 %fusion.4 = s16[2,3,9216]{2,0,1:T(2,128)(2,1)S(1)} fusion(bf16[2,3,9216]{2,0,1:T(2,128)(2,1)} %param.11), kind=kLoop, calls=%fused_computation.9 | loop fusion | flops 1382400 | bytes 221184 | tf_op jit(solution)/shard_map/convert_element_type | solution.py:338
  2.5 0.1 reshape.16
  2.7 7.7 %all_gather.15 = s16[2,432,128]{2,1,0:T(8,128)(2,1)S(1)} all-gather(s16[1,432,128]{2,1,0:T(8,128)(2,1)S(1)} %bitcast.12), channel_id=1, replica_groups=mesh['zl'=2,'core'=2,'y'=4,'x'=4,'zh'=2] {'zh'}, dimensions={0}, use_global_device_ids=true | all-gather | bytes 331776 | tf_op jit(solution)/shard_map/all_gather | solution.py:347
  10.3 33.9 %all-gather.4 = s16[32,432,128]{2,1,0:T(8,128)(2,1)} all-gather(s16[2,432,128]{2,1,0:T(8,128)(2,1)S(1)} %all_gather.15), channel_id=2, replica_groups=mesh['zl'=2,'core'=2,'y'=4,'x'=4,'zh'=2] {'y','x'}, dimensions={0}, use_global_device_ids=true | all-gather | bytes 3760128 | tf_op jit(solution)/shard_map/all_gather | solution.py:348
  44.3 36.7 %pair_coefficients.1 = (s16[8,264,128]{2,1,0:T(8,128)(2,1)}, s16[128,32,128]{2,1,0:T(8,128)(2,1)}) custom-call(s16[32,9,3,16,128]{4,3,2,1,0:T(8,128)(2,1)} %bitcast.11, bf16[8,96,9216]{2,1,0:T(8,128)(2,1)} %refs_2_.1, bf16[8,96,9216]{2,1,0:T(8,128)(2,1)} %refs_2_.1, bf16[4608,256]{1,0:T(8,128)(2,1)} %constant.40.clone.refs_3_, ...), custom_call_target="tpu_custom_call" | custom-call | flops 21743271936 | bytes 41943040 | tf_op jit(solution)/shard_map/pair_coefficients/pallas_call | solution.py:211
  80.9 15.1 %all_to_all.10 = s16[8,264,128]{2,1,0:T(8,128)(2,1)S(1)} all-to-all(s16[8,264,128]{2,1,0:T(8,128)(2,1)} %get-tuple-element.4), channel_id=1, replica_groups=mesh['zl'=2,'core'=2,'y'=4,'x'=4,'zh'=2] {'zh','zl','core'}, dimensions={0} | all-to-all | bytes 1081344 | tf_op jit(solution)/shard_map/all_to_all | solution.py:354
  96.0 5.7 %all-to-all-start.1 = ((s16[128,32,128]{2,1,0:T(8,128)(2,1)}), s16[128,32,128]{2,1,0:T(8,128)(2,1)S(1)}, u32[]{:S(2)}, u32[]{:S(2)}) async-start(s16[128,32,128]{2,1,0:T(8,128)(2,1)} %get-tuple-element.5), calls=%async_computation.1 | async-start | bytes 2097152 | tf_op jit(solution)/shard_map/all_to_all | solution.py:353
  101.6 62.7 %all-gather.5 = s16[128,264,128]{2,1,0:T(8,128)(2,1)} all-gather(s16[8,264,128]{2,1,0:T(8,128)(2,1)S(1)} %all_to_all.10), channel_id=3, replica_groups=mesh['zl'=2,'core'=2,'y'=4,'x'=4,'zh'=2] {'y','x'}, dimensions={0}, use_global_device_ids=true | all-gather | bytes 9191424 | tf_op jit(solution)/shard_map/all_gather | solution.py:355
  164.3 0.0 all-to-all-done.1
  164.3 11.7 %pair_product.1 = (f32[128,1024]{1,0:T(8,128)}, f32[128,1024]{1,0:T(8,128)}) custom-call(s16[16,8,264,128]{3,2,1,0:T(8,128)(2,1)} %bitcast.10, s16[4,16,2,32,128]{4,3,2,1,0:T(8,128)(2,1)S(1)} %bitcast.9), custom_call_target="tpu_custom_call" | custom-call | flops 6442450944 | bytes 12582912 | tf_op jit(solution)/shard_map/pair_product/pallas_call | solution.py:282
  (1 shorter events, 0.0 us)
Async XLA Ops:
  96.0 68.3 %all-to-all-start.1 = ((s16[128,32,128]{2,1,0:T(8,128)(2,1)}), s16[128,32,128]{2,1,0:T(8,128)(2,1)S(1)}, u32[]{:S(2)}, u32[]{:S(2)}) async-start(s16[128,32,128]{2,1,0:T(8,128)(2,1)} %get-tuple-element.5), calls=%async_computation.1 | async-start | bytes 2097152 | tf_op jit(solution)/shard_map/all_to_all | solution.py:353

commit v5 on v4

--- a/solution.py
+++ b/solution.py
@@ -21,6 +21,7 @@
 GROUP = 8
 ROWS = 176
 CODES = 32767.0
+LIFT = 80.0
 LOG2 = math.log(2.0)
 VAL = ("zl", "core")
 COND = ("y", "x", "zh")
@@ -245,7 +246,7 @@
                         [codes[at * height : (at + 1) * height] for at in range(blocks)], axis=1
                     )
                 )
-                scale = -jnp.exp2(2.0 * codes[blocks * height :])
+                scale = -jnp.exp2(2.0 * codes[blocks * height :] + LIFT)
                 block = rows_ref[v, y, h].astype(jnp.float32)
                 block = jnp.concatenate(
                     [block[at * 8 : at * 8 + 8] * scale[:, at : at + 1] for at in range(height // 8)]
@@ -268,8 +269,8 @@
 
     @pl.when(step == pl.num_programs(0) - 1)
     def _():
-        real_ref[...] = total_ref[:rows]
-        imag_ref[...] = total_ref[rows:]
+        real_ref[...] = total_ref[:rows] * 2.0**-LIFT
+        imag_ref[...] = total_ref[rows:] * 2.0**-LIFT
 
 
 def pair_product(cols, rows):

time: 176 us -> 176 us (level)
  no operation moved by 1% of the time
where the time goes in v5:
time: 176 us
  blocking collectives  119 us (68%)
  Pallas kernels  48.3 us (27%)
  starting transfers between devices  5.67 us (3%)
  other arithmetic  1.9 us (1%)
    all_gather x1, blocking collectives, columns_and_rows(): lax.all_gather(line, ('y', 'x'), axis=0)  62.7 us
    pallas_call x1, Pallas kernels, pair_coefficients(): pl.pallas_call(coefficient_kernel, grid=(steps,), in_specs=[vspec, cspec(...  36.7 us
    all_gather x1, blocking collectives, gather_planes(): codes = lax.all_gather(codes, ('y', 'x'), axis=0)  33.9 us
    all_to_all x1, blocking collectives, columns_and_rows(): line = lax.all_to_all(cols, ('zh',) + VAL, 0, 0, tiled=True)  15.1 us
    pallas_call x1, Pallas kernels, pair_product(): pl.pallas_call(pair_kernel, grid=(lines // each,), in_specs=[pl.BlockSpec...  11.7 us
    all_gather x1, blocking collectives, gather_planes(): codes = lax.all_gather(codes, 'zh', axis=0)  7.67 us
    all_to_all x1, starting transfers between devices, columns_and_rows(): sent = lax.all_to_all(rows, VAL + COND, 0, 0, tiled=True)  5.67 us
  transfers between devices with their start and end apart: 1, of which 0 were waited for; matrix products, arithmetic and copies ran while one was open for 0% of the time, Pallas kernels for 0%

profile of v5, /device:TPU:0, one launch (start us, length us, event | category | flops | bytes accessed | tf_op | source)
XLA Modules:
  0.0 176.0 jit_solution(13969551190610551262)
XLA Ops:
  0.6 1.9 %fusion.4 = s16[2,3,9216]{2,0,1:T(2,128)(2,1)S(1)} fusion(bf16[2,3,9216]{2,0,1:T(2,128)(2,1)} %param.11), kind=kLoop, calls=%fused_computation.9 | loop fusion | flops 1382400 | bytes 221184 | tf_op jit(solution)/shard_map/convert_element_type | solution.py:339
  2.5 0.1 reshape.16
  2.7 7.7 %all_gather.15 = s16[2,432,128]{2,1,0:T(8,128)(2,1)S(1)} all-gather(s16[1,432,128]{2,1,0:T(8,128)(2,1)S(1)} %bitcast.12), channel_id=1, replica_groups=mesh['zl'=2,'core'=2,'y'=4,'x'=4,'zh'=2] {'zh'}, dimensions={0}, use_global_device_ids=true | all-gather | bytes 331776 | tf_op jit(solution)/shard_map/all_gather | solution.py:348
  10.3 33.9 %all-gather.4 = s16[32,432,128]{2,1,0:T(8,128)(2,1)} all-gather(s16[2,432,128]{2,1,0:T(8,128)(2,1)S(1)} %all_gather.15), channel_id=2, replica_groups=mesh['zl'=2,'core'=2,'y'=4,'x'=4,'zh'=2] {'y','x'}, dimensions={0}, use_global_device_ids=true | all-gather | bytes 3760128 | tf_op jit(solution)/shard_map/all_gather | solution.py:349
  44.3 36.7 %pair_coefficients.1 = (s16[8,264,128]{2,1,0:T(8,128)(2,1)}, s16[128,32,128]{2,1,0:T(8,128)(2,1)}) custom-call(s16[32,9,3,16,128]{4,3,2,1,0:T(8,128)(2,1)} %bitcast.11, bf16[8,96,9216]{2,1,0:T(8,128)(2,1)} %refs_2_.1, bf16[8,96,9216]{2,1,0:T(8,128)(2,1)} %refs_2_.1, bf16[4608,256]{1,0:T(8,128)(2,1)} %constant.40.clone.refs_3_, ...), custom_call_target="tpu_custom_call" | custom-call | flops 21743271936 | bytes 41943040 | tf_op jit(solution)/shard_map/pair_coefficients/pallas_call | solution.py:212
  80.9 15.1 %all_to_all.10 = s16[8,264,128]{2,1,0:T(8,128)(2,1)S(1)} all-to-all(s16[8,264,128]{2,1,0:T(8,128)(2,1)} %get-tuple-element.4), channel_id=1, replica_groups=mesh['zl'=2,'core'=2,'y'=4,'x'=4,'zh'=2] {'zh','zl','core'}, dimensions={0} | all-to-all | bytes 1081344 | tf_op jit(solution)/shard_map/all_to_all | solution.py:355
  96.0 5.7 %all-to-all-start.1 = ((s16[128,32,128]{2,1,0:T(8,128)(2,1)}), s16[128,32,128]{2,1,0:T(8,128)(2,1)S(1)}, u32[]{:S(2)}, u32[]{:S(2)}) async-start(s16[128,32,128]{2,1,0:T(8,128)(2,1)} %get-tuple-element.5), calls=%async_computation.1 | async-start | bytes 2097152 | tf_op jit(solution)/shard_map/all_to_all | solution.py:354
  101.6 62.7 %all-gather.5 = s16[128,264,128]{2,1,0:T(8,128)(2,1)} all-gather(s16[8,264,128]{2,1,0:T(8,128)(2,1)S(1)} %all_to_all.10), channel_id=3, replica_groups=mesh['zl'=2,'core'=2,'y'=4,'x'=4,'zh'=2] {'y','x'}, dimensions={0}, use_global_device_ids=true | all-gather | bytes 9191424 | tf_op jit(solution)/shard_map/all_gather | solution.py:356
  164.3 0.0 all-to-all-done.1
  164.3 11.7 %pair_product.1 = (f32[128,1024]{1,0:T(8,128)}, f32[128,1024]{1,0:T(8,128)}) custom-call(s16[16,8,264,128]{3,2,1,0:T(8,128)(2,1)} %bitcast.10, s16[4,16,2,32,128]{4,3,2,1,0:T(8,128)(2,1)S(1)} %bitcast.9), custom_call_target="tpu_custom_call" | custom-call | flops 6442450944 | bytes 12582912 | tf_op jit(solution)/shard_map/pair_product/pallas_call | solution.py:283
  (1 shorter events, 0.0 us)
Async XLA Ops:
  96.0 68.3 %all-to-all-start.1 = ((s16[128,32,128]{2,1,0:T(8,128)(2,1)}), s16[128,32,128]{2,1,0:T(8,128)(2,1)S(1)}, u32[]{:S(2)}, u32[]{:S(2)}) async-start(s16[128,32,128]{2,1,0:T(8,128)(2,1)} %get-tuple-element.5), calls=%async_computation.1 | async-start | bytes 2097152 | tf_op jit(solution)/shard_map/all_to_all | solution.py:354

commit v6 on v5

--- a/solution.py
+++ b/solution.py
@@ -117,13 +117,15 @@
     plane_ref, th_ref, tl_ref, index_ref, valence_ref, conduction_ref,
     cols_ref, rows_ref, fold_ref, coef_ref,
 ):
-    th, tl = th_ref[...], tl_ref[...]
+    th = th_ref[...]
+    tables = jnp.concatenate([th, tl_ref[...]])
     used = SIDE * GROUP
     groups = PAIRS // GROUP
     for group in range(groups):
         depth = GROUP * NGRID
         high, low = split(plane_ref[group * depth : (group + 1) * depth])
-        both = dot32(th, high) + dot32(th, low) + dot32(tl, high)
+        first_sums = dot32(tables, high)
+        both = first_sums[: 2 * used] + first_sums[2 * used :] + dot32(th, low)
         cosine, sine = both[:used], both[used:]
         for par in range(2):
             at = par * 256

time: 176 us -> 176 us (level)
  no operation moved by 1% of the time
where the time goes in v6:
time: 176 us
  blocking collectives  119 us (68%)
  Pallas kernels  48.3 us (27%)
  starting transfers between devices  5.66 us (3%)
  other arithmetic  1.9 us (1%)
    all_gather x1, blocking collectives, columns_and_rows(): lax.all_gather(line, ('y', 'x'), axis=0)  62.7 us
    pallas_call x1, Pallas kernels, pair_coefficients(): pl.pallas_call(coefficient_kernel, grid=(steps,), in_specs=[vspec, cspec(...  36.6 us
    all_gather x1, blocking collectives, gather_planes(): codes = lax.all_gather(codes, ('y', 'x'), axis=0)  33.9 us
    all_to_all x1, blocking collectives, columns_and_rows(): line = lax.all_to_all(cols, ('zh',) + VAL, 0, 0, tiled=True)  15.1 us
    pallas_call x1, Pallas kernels, pair_product(): pl.pallas_call(pair_kernel, grid=(lines // each,), in_specs=[pl.BlockSpec...  11.7 us
    all_gather x1, blocking collectives, gather_planes(): codes = lax.all_gather(codes, 'zh', axis=0)  7.67 us
    all_to_all x1, starting transfers between devices, columns_and_rows(): sent = lax.all_to_all(rows, VAL + COND, 0, 0, tiled=True)  5.66 us
  transfers between devices with their start and end apart: 1, of which 0 were waited for; matrix products, arithmetic and copies ran while one was open for 0% of the time, Pallas kernels for 0%

profile of v6, /device:TPU:0, one launch (start us, length us, event | category | flops | bytes accessed | tf_op | source)
XLA Modules:
  0.0 176.0 jit_solution(16422553616293726974)
XLA Ops:
  0.6 1.9 %fusion.4 = s16[2,3,9216]{2,0,1:T(2,128)(2,1)S(1)} fusion(bf16[2,3,9216]{2,0,1:T(2,128)(2,1)} %param.11), kind=kLoop, calls=%fused_computation.9 | loop fusion | flops 1382400 | bytes 221184 | tf_op jit(solution)/shard_map/convert_element_type | solution.py:341
  2.5 0.1 reshape.16
  2.7 7.7 %all_gather.15 = s16[2,432,128]{2,1,0:T(8,128)(2,1)S(1)} all-gather(s16[1,432,128]{2,1,0:T(8,128)(2,1)S(1)} %bitcast.12), channel_id=1, replica_groups=mesh['zl'=2,'core'=2,'y'=4,'x'=4,'zh'=2] {'zh'}, dimensions={0}, use_global_device_ids=true | all-gather | bytes 331776 | tf_op jit(solution)/shard_map/all_gather | solution.py:350
  10.3 33.9 %all-gather.4 = s16[32,432,128]{2,1,0:T(8,128)(2,1)} all-gather(s16[2,432,128]{2,1,0:T(8,128)(2,1)S(1)} %all_gather.15), channel_id=2, replica_groups=mesh['zl'=2,'core'=2,'y'=4,'x'=4,'zh'=2] {'y','x'}, dimensions={0}, use_global_device_ids=true | all-gather | bytes 3760128 | tf_op jit(solution)/shard_map/all_gather | solution.py:351
  44.3 36.6 %pair_coefficients.1 = (s16[8,264,128]{2,1,0:T(8,128)(2,1)}, s16[128,32,128]{2,1,0:T(8,128)(2,1)}) custom-call(s16[32,9,3,16,128]{4,3,2,1,0:T(8,128)(2,1)} %bitcast.11, bf16[8,96,9216]{2,1,0:T(8,128)(2,1)} %refs_2_.1, bf16[8,96,9216]{2,1,0:T(8,128)(2,1)} %refs_2_.1, bf16[4608,256]{1,0:T(8,128)(2,1)} %constant.40.clone.refs_3_, ...), custom_call_target="tpu_custom_call" | custom-call | flops 21743271936 | bytes 41943040 | tf_op jit(solution)/shard_map/pair_coefficients/pallas_call | solution.py:214
  80.9 15.1 %all_to_all.10 = s16[8,264,128]{2,1,0:T(8,128)(2,1)S(1)} all-to-all(s16[8,264,128]{2,1,0:T(8,128)(2,1)} %get-tuple-element.4), channel_id=1, replica_groups=mesh['zl'=2,'core'=2,'y'=4,'x'=4,'zh'=2] {'zh','zl','core'}, dimensions={0} | all-to-all | bytes 1081344 | tf_op jit(solution)/shard_map/all_to_all | solution.py:357
  95.9 5.7 %all-to-all-start.1 = ((s16[128,32,128]{2,1,0:T(8,128)(2,1)}), s16[128,32,128]{2,1,0:T(8,128)(2,1)S(1)}, u32[]{:S(2)}, u32[]{:S(2)}) async-start(s16[128,32,128]{2,1,0:T(8,128)(2,1)} %get-tuple-element.5), calls=%async_computation.1 | async-start | bytes 2097152 | tf_op jit(solution)/shard_map/all_to_all | solution.py:356
  101.6 62.7 %all-gather.5 = s16[128,264,128]{2,1,0:T(8,128)(2,1)} all-gather(s16[8,264,128]{2,1,0:T(8,128)(2,1)S(1)} %all_to_all.10), channel_id=3, replica_groups=mesh['zl'=2,'core'=2,'y'=4,'x'=4,'zh'=2] {'y','x'}, dimensions={0}, use_global_device_ids=true | all-gather | bytes 9191424 | tf_op jit(solution)/shard_map/all_gather | solution.py:358
  164.3 0.0 all-to-all-done.1
  164.3 11.7 %pair_product.1 = (f32[128,1024]{1,0:T(8,128)}, f32[128,1024]{1,0:T(8,128)}) custom-call(s16[16,8,264,128]{3,2,1,0:T(8,128)(2,1)} %bitcast.10, s16[4,16,2,32,128]{4,3,2,1,0:T(8,128)(2,1)S(1)} %bitcast.9), custom_call_target="tpu_custom_call" | custom-call | flops 6442450944 | bytes 12582912 | tf_op jit(solution)/shard_map/pair_product/pallas_call | solution.py:285
  (1 shorter events, 0.0 us)
Async XLA Ops:
  95.9 68.3 %all-to-all-start.1 = ((s16[128,32,128]{2,1,0:T(8,128)(2,1)}), s16[128,32,128]{2,1,0:T(8,128)(2,1)S(1)}, u32[]{:S(2)}, u32[]{:S(2)}) async-start(s16[128,32,128]{2,1,0:T(8,128)(2,1)} %get-tuple-element.5), calls=%async_computation.1 | async-start | bytes 2097152 | tf_op jit(solution)/shard_map/all_to_all | solution.py:356
